TPU v7x, 32 devices: a whole 2x2x4 slice. The times are simulated.
32 devices in a mesh: mod: 2 (over y), batch: 16 (over z, x, core).
Axes of the slice: x: 2, y: 2, z: 4, core: 2. Of those that a mesh axis runs over, the one named last changes fastest.
Arguments:
- tokens: bfloat16 [64, 256, 768], P('batch', 'mod'), may hold values from -6 to 6
- caption_lengths: int32 [64], P('batch'), may hold values from 8 to 128, as said below
- region_mask: int32 [64, 128], P('batch'), may hold values from 0 to 1, as said below
- w_qkv: bfloat16 [768, 2304], replicated, may hold values from -0.21875 to 0.21875
- query_bias: float32 [768], replicated, may hold values from -1.5 to 1.5
- value_bias: float32 [768], replicated, may hold values from -1.5 to 1.5
- w_out: bfloat16 [768, 768], replicated, may hold values from -0.875 to 0.875
- out_bias: float32 [768], replicated, may hold values from -1.5 to 1.5
- w_up: bfloat16 [768, 3072], replicated, may hold values from -0.21875 to 0.21875
- up_bias: float32 [3072], replicated, may hold values from -1.5 to 1.5
- w_down: bfloat16 [3072, 768], replicated, may hold values from -0.109375 to 0.109375
- down_bias: float32 [768], replicated, may hold values from -1.5 to 1.5
- gain_one: float32 [768], replicated, may hold values from 0.5 to 1.5
- shift_one: float32 [768], replicated, may hold values from -1.5 to 1.5
- gain_two: float32 [768], replicated, may hold values from 0.5 to 1.5
- shift_two: float32 [768], replicated, may hold values from -1.5 to 1.5
- cotangent: bfloat16 [64, 256, 768], P('batch', 'mod'), may hold values from -6 to 6
Outputs:
- layer_output: bfloat16 [64, 256, 768], P('batch', 'mod')
- input_grad: float32 [64, 256, 768], P('batch', 'mod')
- grad_qkv: float32 [768, 2304], replicated
- grad_query_bias: float32 [768], replicated
- grad_value_bias: float32 [768], replicated
- grad_out: float32 [768, 768], replicated
- grad_out_bias: float32 [768], replicated
- grad_up: float32 [768, 3072], replicated
- grad_up_bias: float32 [3072], replicated
- grad_down: float32 [3072, 768], replicated
- grad_down_bias: float32 [768], replicated
- grad_gain_one: float32 [768], replicated
- grad_shift_one: float32 [768], replicated
- grad_gain_two: float32 [768], replicated
- grad_shift_two: float32 [768], replicated
Inputs may be any that keep to these rules, and one draw needn't show every extreme that they name: `caption_lengths`: every caption has 8 to 128 true tokens; some caption has exactly 128 and some exactly 8. `region_mask`: every item has exactly 100 valid regions among its 128 region slots.
All inputs are finite; a program needn't handle non-finite values.
Results may differ from a plain program's by a relative error of at most 0.014.
Values may be sent and summed in bfloat16 or wider, within the bound.
No kernel may reach another device: no remote copies, remote signals or barrier semaphores. Data moves between devices by JAX's collectives and lax.ppermute only.
A program may use at most 192 MiB of HBM per device.

v0:
```python
import jax
import jax.numpy as jnp
from jax import lax
from jax.sharding import PartitionSpec as P

HEADS = 12
HEAD_DIM = 64
FF = 3072
SLOTS = 128


EPSILON = 1e-12


def multiply(left, right):
    return jnp.dot(left, right, preferred_element_type=jnp.float32)


def across_rows(left, right):
    return lax.dot_general(
        left, right, (((0,), (0,)), ((), ())), preferred_element_type=jnp.float32
    )


def against_rows(left, right):
    return lax.dot_general(
        left, right, (((1,), (1,)), ((), ())), preferred_element_type=jnp.float32
    )


def norm_forward(values_in, gain, shift):
    center = jnp.mean(values_in, axis=-1, keepdims=True)
    centered = values_in - center
    variance = jnp.mean(centered * centered, axis=-1, keepdims=True)
    inverse = lax.rsqrt(variance + EPSILON)
    scaled = centered * inverse
    return (scaled * gain + shift, scaled, inverse)


def norm_backward(grad_result, scaled, inverse, gain):
    grad_scaled = grad_result * gain
    first_mean = jnp.mean(grad_scaled, axis=-1, keepdims=True)
    second_mean = jnp.mean(grad_scaled * scaled, axis=-1, keepdims=True)
    grad_in = inverse * (grad_scaled - first_mean - scaled * second_mean)
    return (grad_in, jnp.sum(grad_result * scaled, axis=0), jnp.sum(grad_result, axis=0))


def gelu_slope(upward):
    normal_cdf = 0.5 * (1.0 + lax.erf(upward * 0.7071067811865476))
    density = jnp.exp(-0.5 * upward * upward) * 0.3989422804014327
    return normal_cdf + upward * density


def local(
    tokens,
    caption_lengths,
    region_mask,
    w_qkv,
    query_bias,
    value_bias,
    w_out,
    out_bias,
    w_up,
    up_bias,
    w_down,
    down_bias,
    gain_one,
    shift_one,
    gain_two,
    shift_two,
    cotangent,
):
    item_count, slot_count, width = tokens.shape
    rows_total = item_count * slot_count
    scale = HEAD_DIM ** (-0.5)
    shaped = (item_count, slot_count, HEADS, HEAD_DIM)
    joint_shape = (item_count, 2 * slot_count, HEADS, HEAD_DIM)
    flat = tokens.reshape(rows_total, width)
    joined = multiply(flat, w_qkv)
    queries = (joined[:, :width] + query_bias).astype(jnp.bfloat16)
    keys = joined[:, width : 2 * width].astype(jnp.bfloat16)
    values = (joined[:, 2 * width :] + value_bias).astype(jnp.bfloat16)
    keys_all, values_all = (
        lax.all_gather(keys.reshape(item_count, slot_count, width), "mod", axis=1, tiled=True),
        lax.all_gather(values.reshape(item_count, slot_count, width), "mod", axis=1, tiled=True),
    )
    query_heads = queries.reshape(shaped)
    key_heads = keys_all.reshape(joint_shape)
    value_heads = values_all.reshape(joint_shape)
    slot_index = lax.broadcasted_iota(jnp.int32, (item_count, SLOTS), 1)
    text_valid = slot_index < caption_lengths[:, None]
    key_valid = jnp.concatenate([text_valid, region_mask > 0], axis=1)

    def scores_of():
        raw = (
            jnp.einsum(
                "ishd,ijhd->ihsj", query_heads, key_heads, preferred_element_type=jnp.float32
            )
            * scale
        )
        return jnp.where(key_valid[:, None, None, :], raw, -1e30)

    scores = scores_of()
    highest = jnp.max(scores, axis=-1, keepdims=True)
    exponent = jnp.exp(scores - highest)
    expsum = jnp.sum(exponent, axis=-1, keepdims=True)
    probs = exponent / expsum
    log_total = highest + jnp.log(expsum)
    attended = jnp.einsum(
        "ihsj,ijhd->ishd",
        probs.astype(jnp.bfloat16),
        value_heads,
        preferred_element_type=jnp.float32,
    )
    attended = attended.reshape(rows_total, width).astype(jnp.bfloat16)
    branch = multiply(attended, w_out) + out_bias
    normed, scaled_one, inverse_one = norm_forward(
        flat.astype(jnp.float32) + branch, gain_one, shift_one
    )
    normed_low = normed.astype(jnp.bfloat16)
    upward = multiply(normed_low, w_up) + up_bias
    activated = jax.nn.gelu(upward, approximate=False).astype(jnp.bfloat16)
    down_branch = multiply(activated, w_down) + down_bias
    result, scaled_two, inverse_two = norm_forward(normed + down_branch, gain_two, shift_two)
    layer_output = result.astype(jnp.bfloat16).reshape(item_count, slot_count, width)
    grad_result = cotangent.reshape(rows_total, width).astype(jnp.float32)
    grad_second, grad_gain_two, grad_shift_two = norm_backward(
        grad_result, scaled_two, inverse_two, gain_two
    )
    grad_down_low = grad_second.astype(jnp.bfloat16)
    grad_down_bias = jnp.sum(grad_down_low, axis=0, dtype=jnp.float32)
    grad_down = across_rows(activated, grad_down_low)
    grad_upward = (against_rows(grad_down_low, w_down) * gelu_slope(upward)).astype(jnp.bfloat16)
    grad_up_bias = jnp.sum(grad_upward, axis=0, dtype=jnp.float32)
    grad_up = across_rows(normed_low, grad_upward)
    grad_normed = grad_second + against_rows(grad_upward, w_up)
    grad_first, grad_gain_one, grad_shift_one = norm_backward(
        grad_normed, scaled_one, inverse_one, gain_one
    )
    grad_branch = grad_first.astype(jnp.bfloat16)
    grad_out_bias = jnp.sum(grad_branch, axis=0, dtype=jnp.float32)
    grad_out = across_rows(attended, grad_branch)
    grad_attended = against_rows(grad_branch, w_out).astype(jnp.bfloat16).reshape(shaped)
    probs_again = jnp.exp(scores_of() - log_total)
    probs_low = probs_again.astype(jnp.bfloat16)
    grad_values_part = jnp.einsum(
        "ihsj,ishd->ijhd", probs_low, grad_attended, preferred_element_type=jnp.float32
    )
    grad_probs = jnp.einsum(
        "ishd,ijhd->ihsj", grad_attended, value_heads, preferred_element_type=jnp.float32
    )
    inner = jnp.sum(probs_again * grad_probs, axis=-1, keepdims=True)
    grad_scores = (probs_again * (grad_probs - inner)).astype(jnp.bfloat16)
    grad_queries = (
        jnp.einsum("ihsj,ijhd->ishd", grad_scores, key_heads, preferred_element_type=jnp.float32)
        * scale
    ).astype(jnp.bfloat16)
    grad_keys_part = (
        jnp.einsum("ihsj,ishd->ijhd", grad_scores, query_heads, preferred_element_type=jnp.float32)
        * scale
    )
    grad_keys, grad_values = (
        lax.psum_scatter(
            grad_keys_part.reshape(item_count, 2 * slot_count, width).astype(jnp.bfloat16),
            "mod",
            scatter_dimension=1,
            tiled=True,
        ).astype(jnp.float32),
        lax.psum_scatter(
            grad_values_part.reshape(item_count, 2 * slot_count, width).astype(jnp.bfloat16),
            "mod",
            scatter_dimension=1,
            tiled=True,
        ).astype(jnp.float32),
    )
    grad_queries = grad_queries.reshape(rows_total, width)
    grad_keys = grad_keys.reshape(rows_total, width).astype(jnp.bfloat16)
    grad_values = grad_values.reshape(rows_total, width).astype(jnp.bfloat16)
    grad_joined = jnp.concatenate([grad_queries, grad_keys, grad_values], axis=1)
    grad_qkv = across_rows(flat, grad_joined)
    grad_query_bias = jnp.sum(grad_queries, axis=0, dtype=jnp.float32)
    grad_value_bias = jnp.sum(grad_values, axis=0, dtype=jnp.float32)
    input_grad = (grad_first + against_rows(grad_joined, w_qkv)).reshape(
        item_count, slot_count, width
    )
    small_stack = jnp.stack(
        [
            grad_query_bias,
            grad_value_bias,
            grad_out_bias,
            grad_down_bias,
            grad_gain_one,
            grad_shift_one,
            grad_gain_two,
            grad_shift_two,
        ]
    ).reshape(-1)
    share_qkv, share_out, share_up, share_down, share_upb, share_small = (
        lax.psum_scatter(grad_qkv.reshape(-1), ("mod", "batch"), scatter_dimension=0, tiled=True),
        lax.psum_scatter(grad_out.reshape(-1), ("mod", "batch"), scatter_dimension=0, tiled=True),
        lax.psum_scatter(grad_up.reshape(-1), ("mod", "batch"), scatter_dimension=0, tiled=True),
        lax.psum_scatter(grad_down.reshape(-1), ("mod", "batch"), scatter_dimension=0, tiled=True),
        lax.psum_scatter(grad_up_bias, ("mod", "batch"), scatter_dimension=0, tiled=True),
        lax.psum_scatter(small_stack, ("mod", "batch"), scatter_dimension=0, tiled=True),
    )
    total_qkv, total_out, total_up, total_down, total_upb, total_small = (
        lax.all_gather(share_qkv.astype(jnp.bfloat16), ("mod", "batch"), axis=0, tiled=True).astype(
            share_qkv.dtype
        ),
        lax.all_gather(share_out.astype(jnp.bfloat16), ("mod", "batch"), axis=0, tiled=True).astype(
            share_out.dtype
        ),
        lax.all_gather(share_up.astype(jnp.bfloat16), ("mod", "batch"), axis=0, tiled=True).astype(
            share_up.dtype
        ),
        lax.all_gather(
            share_down.astype(jnp.bfloat16), ("mod", "batch"), axis=0, tiled=True
        ).astype(share_down.dtype),
        lax.all_gather(share_upb.astype(jnp.bfloat16), ("mod", "batch"), axis=0, tiled=True).astype(
            share_upb.dtype
        ),
        lax.all_gather(
            share_small.astype(jnp.bfloat16), ("mod", "batch"), axis=0, tiled=True
        ).astype(share_small.dtype),
    )
    small_rows = total_small.reshape(8, width)
    return (
        layer_output,
        input_grad,
        total_qkv.reshape(width, 3 * width),
        small_rows[0],
        small_rows[1],
        total_out.reshape(width, width),
        small_rows[2],
        total_up.reshape(width, FF),
        total_upb,
        total_down.reshape(FF, width),
        small_rows[3],
        small_rows[4],
        small_rows[5],
        small_rows[6],
        small_rows[7],
    )


def solution(mesh):
    return jax.shard_map(
        local,
        mesh=mesh,
        in_specs=(
            P("batch", "mod", None),
            P("batch"),
            P("batch", None),
            P(),
            P(),
            P(),
            P(),
            P(),
            P(),
            P(),
            P(),
            P(),
            P(),
            P(),
            P(),
            P(),
            P("batch", "mod", None),
        ),
        out_specs=(
            P("batch", "mod", None),
            P("batch", "mod", None),
            P(),
            P(),
            P(),
            P(),
            P(),
            P(),
            P(),
            P(),
            P(),
            P(),
            P(),
            P(),
            P(),
        ),
        check_vma=False,
    )
```

profile of v0, /device:TPU:0, one launch (start us, length us, event | category | flops | bytes accessed | tf_op | source)
XLA Modules:
  0.0 951.6 jit_solution(13652980306815861040)
XLA Ops:
  9.2 3.2 fusion.63
  15.6 3.3 fusion.25
  26.6 19.0 %all-gather.9.cloned.1.call-done = bf16[4,256,768]{2,1,0:T(8,128)(2,1)} async-done(((bf16[4,128,768]{2,1,0:T(8,128)(2,1)}), bf16[4,256,768]{2,1,0:T(8,128)(2,1)}) %all-gather.9.cloned.1.call-update) | async-done | bytes 1572880 | tf_op jit(solution)/shard_map/all_gather | solution.py:84
  48.2 3.4 fusion.60
  55.5 19.4 %all-gather.7.cloned.1.call-done = bf16[4,256,768]{2,1,0:T(8,128)(2,1)} async-done(((bf16[4,128,768]{2,1,0:T(8,128)(2,1)}), bf16[4,256,768]{2,1,0:T(8,128)(2,1)}) %all-gather.7.cloned.1.call-update) | async-done | bytes 1572880 | tf_op jit(solution)/shard_map/all_gather | solution.py:85
  77.5 4.7 fusion.36
  84.3 19.3 %fusion.2 = (bf16[512,3072]{1,0:T(8,128)(2,1)S(1)}, f32[512,3072]{1,0:T(8,128)S(1)}) fusion(f32[3072]{0:T(1024)S(1)} %copy-done.32, bf16[768,3072]{1,0:T(8,128)(2,1)} %param.25, f32[512,768]{1,0:T(8,128)S(1)} %get-tuple-element.49, f32[768]{0:T(1024)S(1)} %copy-done.35, f32[768]{0:T(1024)S(1)} %copy-done.26, f32[512]{0:T(512)S(1)} %add_rsqrt_fusion.1, ...), kind=kOutput, calls=%fused_computation.4 | convolution fusion | flops 2521694208 | bytes 15751168 | tf_op jit(solution)/shard_map/dot_general | solution.py:16
  110.3 5.3 convert_reduce_fusion
  115.5 3.6 multiply_reduce_fusion.1
  127.9 5.3 fusion.22
  135.9 5.9 multiply_reduce_fusion
  141.8 4.7 multiply_convert_fusion
  152.0 3.7 convert_reduce_fusion.5
  163.7 3.8 fusion.38
  167.5 3.4 reshape.217
  171.0 5.3 convolution_bitcast_fusion.1
  176.3 6.0 copy.70
  182.2 5.2 fusion.52
  187.4 10.8 %reshape.223 = f32[2359296]{0:T(1024)} reshape(f32[3072,768]{1,0:T(8,128)} %fusion.52) | data formatting | bytes 18874368 | tf_op jit(solution)/shard_map/reshape | solution.py:202
  202.9 6.8 convolution_bitcast_fusion
  209.7 8.0 copy.67
  217.7 7.9 reshape.213
  230.2 456.5 %all-reduce.11 = (bf16[1769472]{0:T(1024)(128)(2,1)}, bf16[6144]{0:T(1024)(128)(2,1)}, bf16[589824]{0:T(1024)(128)(2,1)}, bf16[2359296]{0:T(1024)(128)(2,1)}, bf...) all-reduce(f32[1769472]{0:T(1024)} %reshape.213, ...), channel_id=4, replica_groups=mesh['mod'=2,'batch'=16] {'mod','batch'}, use_global_device_ids=true, to_apply=%region_13.14.clone | all-reduce | flops 7087104 | bytes 42522624
  698.0 39.5 %all-reduce.9 = (bf16[6144]{0:T(1024)(128)(2,1)S(1)}, bf16[3072]{0:T(1024)(128)(2,1)}) all-reduce(bf16[6144]{0:T(1024)(128)(2,1)} %copy-done.16, bf16[3072]{0:T(1024)(128)(2,1)} %dynamic-update-slice.1), channel_id=1, replica_groups=mesh['mod'=2,'batch'=16] {'mod','batch'}, use_global_device_ids=true, to_apply=%add | all-reduce | flops 9216 | bytes 36864
  739.4 5.3 convolution_add_fusion
  744.7 3.3 reshape.230
  748.1 55.1 %all-gather.11.cloned.1.call-done = bf16[1769472]{0:T(1024)(128)(2,1)} async-done(((bf16[55296]{0:T(1024)(128)(2,1)}), bf16[1769472]{0:T(1024)(128)(2,1)}) %all-gather.11.cloned.1.call-update) | async-done | bytes 3538960 | tf_op jit(solution)/shard_map/all_gather | solution.py:207
  803.2 7.9 reshape.228
  811.1 57.9 %all-gather.15.cloned.1.call-done = bf16[2359296]{0:T(1024)(128)(2,1)} async-done(((bf16[73728]{0:T(1024)(128)(2,1)}), bf16[2359296]{0:T(1024)(128)(2,1)}) %all-gather.15.cloned.1.call-update) | async-done | bytes 4718608 | tf_op jit(solution)/shard_map/all_gather | solution.py:213
  869.1 8.7 reshape.232
  877.8 56.6 %all-gather.17.cloned.1.call-done = bf16[2359296]{0:T(1024)(128)(2,1)} async-done(((bf16[73728]{0:T(1024)(128)(2,1)}), bf16[2359296]{0:T(1024)(128)(2,1)}) %all-gather.17.cloned.1.call-update) | async-done | bytes 4718608 | tf_op jit(solution)/shard_map/all_gather | solution.py:216
  934.4 10.0 %reshape.234 = f32[3072,768]{1,0:T(8,128)} reshape(bf16[2359296]{0:T(1024)(128)(2,1)} %all-gather.17.cloned.1.call-done) | data formatting | bytes 14155776 | tf_op jit(solution)/shard_map/reshape | solution.py:237
  (164 shorter events, 77.5 us)
Async XLA Ops:
  7.2 38.4 %all-gather.9.cloned.1.call-start = ((), (), s32[]{:S(2)}) async-start(), calls=%async_computation.3 | async-start | bytes 2359296 | tf_op jit(solution)/shard_map/all_gather | solution.py:84
  9.2 6.4 copy-start.24
  9.2 6.4 copy-start.25
  15.5 59.4 %all-gather.7.cloned.1.call-start = ((), (), s32[]{:S(2)}) async-start(), calls=%async_computation.2 | async-start | bytes 2359296 | tf_op jit(solution)/shard_map/all_gather | solution.py:85
  18.9 5.6 copy-start.17
  18.9 179.4 %reduce-scatter.5.cloned.1.call-start = ((), (), s32[]{:S(2)}) async-start(), calls=%async_computation.5 | async-start | bytes 2359296 | tf_op jit(solution)/shard_map/reduce_scatter | solution.py:169
  77.5 5.4 copy-start.30
  77.5 5.4 copy-start.31
  77.5 5.4 copy-start.33
  83.0 20.7 %slice-start = ((s8[4718592]{0:T(1024)(128)(4,1)}), s8[4194304]{0:T(1024)(128)(4,1)S(1)}, s32[]{:S(2)}) async-start(s8[4718592]{0:T(1024)(128)(4,1)} %bitcast.101), calls=%async_computation.10 | async-start | bytes 8388608
  83.9 35.3 %copy-start.7 = (f32[512,768]{1,0:T(8,128)}, f32[512,768]{1,0:T(8,128)S(1)}, u32[]{:S(2)}) copy-start(f32[512,768]{1,0:T(8,128)S(1)} %get-tuple-element.49) | copy-start | bytes 4718596
  84.3 34.9 %copy-start.21 = (f32[512]{0:T(512)}, f32[512]{0:T(512)S(1)}, u32[]{:S(2)}) copy-start(f32[512]{0:T(512)S(1)} %add_rsqrt_fusion.1) | copy-start | bytes 6148
  84.3 19.4 %slice-start.1 = ((s8[4718592]{0:T(1024)(128)(4,1)}), s8[524288]{0:T(1024)(128)(4,1)S(1)}, s32[]{:S(2)}) async-start(s8[4718592]{0:T(1024)(128)(4,1)} %bitcast.101), calls=%async_computation.11 | async-start | bytes 1048576
  84.3 19.4 %copy-start.34 = (f32[768]{0:T(1024)S(1)}, f32[768]{0:T(1024)}, u32[]{:S(2)}) copy-start(f32[768]{0:T(1024)} %param.28) | copy-start | bytes 9220
  108.1 7.4 slice-start.2
  110.3 5.3 copy-start.5
  110.3 5.3 slice-start.3
  115.5 3.7 copy-start.37
  135.8 64.7 %reduce-scatter.3.cloned.1.call-start = ((), (), s32[]{:S(2)}) async-start(), calls=%async_computation.4 | async-start | bytes 2359296 | tf_op jit(solution)/shard_map/reduce_scatter | solution.py:163
  135.9 5.9 copy-start.13
  141.8 4.7 copy-start.3
  151.3 593.4 %all-gather.13.cloned.1.call-start = ((), (), s32[]{:S(2)}) async-start(), calls=%async_computation.7 | async-start | bytes 1216512 | tf_op jit(solution)/shard_map/all_gather | solution.py:210
  152.0 11.1 %copy-start.18 = (f32[768]{0:T(1024)S(1)}, f32[768]{0:T(1024)}, u32[]{:S(2)}) copy-start(f32[768]{0:T(1024)} %get-tuple-element.17) | copy-start | bytes 9220
  167.5 3.5 copy-start.27
  167.5 3.5 copy-start.36
  176.2 6.0 copy-start.6
  176.2 6.0 copy-start.11
  217.6 9.8 %copy-start.20 = (f32[1,768]{1,0:T(1,128)S(1)}, f32[1,768]{1,0:T(1,128)}, u32[]{:S(2)}) copy-start(f32[1,768]{1,0:T(1,128)} %stack.34) | copy-start | bytes 9220
  217.7 12.6 %copy-start.19 = (f32[3072]{0:T(1024)S(1)}, f32[3072]{0:T(1024)}, u32[]{:S(2)}) copy-start(f32[3072]{0:T(1024)} %get-tuple-element.59) | copy-start | bytes 36868
  688.1 115.1 %all-gather.11.cloned.1.call-start = ((), (), s32[]{:S(2)}) async-start(), calls=%async_computation.6 | async-start | bytes 3649536 | tf_op jit(solution)/shard_map/all_gather | solution.py:207
  689.8 179.3 %all-gather.15.cloned.1.call-start = ((), (), s32[]{:S(2)}) async-start(), calls=%async_computation.8 | async-start | bytes 4866048 | tf_op jit(solution)/shard_map/all_gather | solution.py:213
  691.4 243.0 %all-gather.17.cloned.1.call-start = ((), (), s32[]{:S(2)}) async-start(), calls=%async_computation.9 | async-start | bytes 4866048 | tf_op jit(solution)/shard_map/all_gather | solution.py:216
  (18 other events, 35.3 us)
Sparse Core Ops, SparseCore 0:
  15.7 29.8 all-gather.8
  47.7 27.2 all-gather.6
  135.9 26.0 reduce-scatter.4
  164.2 26.0 reduce-scatter.2
  688.2 52.6 all-gather.12
  744.3 58.8 all-gather.10
  806.6 62.3 all-gather.14
  871.9 62.3 all-gather.16
where the time goes:
time: 960 us; the launch traced here: 952 us
  blocking collectives  496 us (52%)
  waiting for transfers between devices  208 us (22%)
  local copies, waits for them, and re-layouts  122 us (13%)
  matrix products  88.5 us (9%)
  other arithmetic  21 us (2%)
  between operations  15.1 us (2%)
    unnamed x2, blocking collectives  496 us
    all_gather x1, waiting for transfers between devices, local(): lax.all_gather(share_up.astype(jnp.bfloat16), ('mod', 'batch'), axis=0, t...  57.9 us
    all_gather x1, waiting for transfers between devices, local(): lax.all_gather(share_down.astype(jnp.bfloat16), ('mod', 'batch'), axis=0,...  56.6 us
    all_gather x1, waiting for transfers between devices, local(): lax.all_gather(share_qkv.astype(jnp.bfloat16), ('mod', 'batch'), axis=0,...  55.1 us
    dot_general x4, matrix products, multiply(): return jnp.dot(left, right, preferred_element_type=jnp.float32)  26.2 us
    unnamed x96, local copies, waits for them, and re-layouts  24.8 us
    dot_general x4, matrix products, across_rows(): lax.dot_general(left, right, (((0,), (0,)), ((), ())), preferred_element_...  21.1 us
    all_gather x1, waiting for transfers between devices, local(): lax.all_gather(values.reshape(item_count, slot_count, width), 'mod', axis...  19.4 us
  transfers between devices with their start and end apart: 8, of which 5 were waited for; matrix products, arithmetic and copies ran while one was open for 13% of the time, Pallas kernels for 0%

commit v1 on v0

v1 whole, which is shorter than its diff:
```python
import functools

import jax
import jax.numpy as jnp
from jax import lax
from jax.experimental import pallas as pl
from jax.experimental.pallas import tpu as pltpu
from jax.sharding import PartitionSpec as P

HEADS = 12
HEAD_DIM = 64
WIDTH = 768
FF = 3072
SLOTS = 128
EPSILON = 1e-12
PAIR = 2 * HEAD_DIM
HALF = WIDTH // 2
FF_HALF = FF // 2
CHUNK = 768
CHUNKS = FF // CHUNK
MASKED = -1e30
SCALE = HEAD_DIM ** (-0.5)
MIB = 1 << 20

BF16 = jnp.bfloat16
F32 = jnp.float32


def nn(left, right):
    return lax.dot_general(left, right, (((1,), (0,)), ((), ())), preferred_element_type=F32)


def nt(left, right):
    return lax.dot_general(left, right, (((1,), (1,)), ((), ())), preferred_element_type=F32)


def tn(left, right):
    return lax.dot_general(left, right, (((0,), (0,)), ((), ())), preferred_element_type=F32)


def whole(shape):
    zeros = (0,) * len(shape)
    return pl.BlockSpec(shape, lambda *_: zeros, pipeline_mode=pl.Buffered(1))


TOKEN = (8, 128)
RATE = 10e9


def run(
    body, name, pos, grid, inputs, outputs, us, mib, after=(), scratch=(), aliases={}, carry=()
):
    tokens = len(after)
    riders = len(carry)
    first = 1 + len(inputs)
    outs = first + tokens + riders
    last = outs + len(outputs)
    extra = 2 if carry else 1

    def wrapped(*refs):
        refs[last][...] = jnp.zeros(TOKEN, F32)
        if carry:
            added = [ref[...] for ref in refs[first + tokens : outs]]
            refs[last + 1][...] = sum(added[1:], added[0])
        body(*refs[:first], *refs[outs:last], *refs[last + extra :])

    whole_of = lambda a: whole(a.shape)
    out = pl.pallas_call(
        wrapped,
        grid_spec=pltpu.PrefetchScalarGridSpec(
            num_scalar_prefetch=1,
            grid=grid,
            in_specs=[spec for _, spec in inputs]
            + [pl.BlockSpec(memory_space=pl.ANY)] * tokens
            + [whole_of(a) for a in carry],
            out_specs=[spec for _, _, spec in outputs]
            + [whole(TOKEN)]
            + [whole_of(a) for a in carry[:1]],
            scratch_shapes=list(scratch),
        ),
        out_shape=[jax.ShapeDtypeStruct(shape, kind) for shape, kind, _ in outputs]
        + [jax.ShapeDtypeStruct(TOKEN, F32)]
        + [jax.ShapeDtypeStruct(a.shape, F32) for a in carry[:1]],
        compiler_params=pltpu.CompilerParams(
            dimension_semantics=("arbitrary",) * len(grid), vmem_limit_bytes=mib * MIB
        ),
        cost_estimate=pl.CostEstimate(
            flops=int(us * RATE), bytes_accessed=1000, transcendentals=0
        ),
        input_output_aliases=aliases,
        name=name,
    )(pos, *[array for array, _ in inputs], *after, *carry)
    if carry:
        return out[:-2], out[-2], out[-1]
    return out[:-1], out[-1]


def lane_half(shape):
    return lax.broadcasted_iota(jnp.int32, shape, 1) >= HEAD_DIM


def head_operands(upper, head, query, key, ones, mask):
    if head == 0:
        return jnp.where(upper, ones, query), jnp.where(upper, mask, key)
    return jnp.where(upper, query, ones), jnp.where(upper, key, mask)


def softmax_over_keys(scores):
    exponent = jnp.exp(scores - jnp.max(scores, axis=0, keepdims=True))
    return exponent * (1.0 / jnp.sum(exponent, axis=0, keepdims=True))


def norm(rows):
    center = jnp.mean(rows, axis=-1, keepdims=True)
    centered = rows - center
    variance = jnp.mean(centered * centered, axis=-1, keepdims=True)
    inverse = lax.rsqrt(variance + EPSILON)
    return centered * inverse, inverse


def norm_back(grad_result, scaled, inverse, gain):
    grad_scaled = grad_result * gain
    first_mean = jnp.mean(grad_scaled, axis=-1, keepdims=True)
    second_mean = jnp.mean(grad_scaled * scaled, axis=-1, keepdims=True)
    return inverse * (grad_scaled - first_mean - scaled * second_mean)


GROUP = 384
GROUPS = WIDTH // GROUP
FORWARD = GROUPS
BACKWARD = GROUPS + CHUNKS
STEPS = GROUPS + 2 * CHUNKS
PARTS = 1


def gelu_and_slope(upward):
    size = jnp.abs(upward)
    divisor = 1.0 + (0.3275911 * 0.7071067811865476) * size
    near = pl.reciprocal(divisor, approx=True)
    near = near * (2.0 - divisor * near)
    bell = jnp.exp(-0.5 * upward * upward)
    poly = 0.5 * 1.061405429 * near - 0.5 * 1.453152027
    poly = poly * near + 0.5 * 1.421413741
    poly = poly * near - 0.5 * 0.284496736
    poly = poly * near + 0.5 * 0.254829592
    tail = poly * near * bell
    phi = jnp.where(upward >= 0, 1.0 - tail, tail)
    return upward * phi, phi + upward * (bell * 0.3989422804014327)


def layer_body(
    items,
    pos,
    own,
    other,
    mask,
    ones,
    w_q,
    w_k,
    w_v,
    query_bias,
    value_bias,
    w_out,
    out_bias,
    gain_one,
    shift_one,
    w_up,
    up_bias,
    w_down,
    down_bias,
    gain_two,
    shift_two,
    cot_own,
    cot_other,
    queries,
    keys,
    values,
    keep,
    act_mine,
    send,
    out_own,
    out_other,
    up_theirs,
    up_mine,
    up_bias_grad,
    grad_first,
    branch_theirs,
    branch_mine,
    grad_attended,
    small,
    total,
    attended,
    slope,
    normed,
    scaled,
    inverse,
    grad_second,
    branch,
):
    step = pl.program_id(0)
    span = 2 * SLOTS
    count = items * span
    rows_out = keep.at[0]
    part = count // PARTS
    parts = [slice(i * part, (i + 1) * part) for i in range(PARTS)]

    @pl.when(step == 0)
    def _():
        for item in range(items):
            rows_out[item * span : item * span + SLOTS, :] = own[item]
            rows_out[item * span + SLOTS : (item + 1) * span, :] = other[item]
        total[...] = jnp.zeros_like(total)

    @pl.when(step < FORWARD)
    def _():
        rows = rows_out[...]
        queries[...] = (nn(rows, w_q[...]) + query_bias[...]).astype(BF16)
        keys[...] = nn(rows, w_k[...]).astype(BF16)
        values[...] = (nn(rows, w_v[...]) + value_bias[...]).astype(BF16)
        upper = lane_half((span, PAIR))
        for item in range(items):
            at = slice(item * span, (item + 1) * span)
            for pair in range(GROUP // PAIR):
                cols = slice(pair * PAIR, (pair + 1) * PAIR)
                query = queries[at, cols] * jnp.asarray(SCALE, BF16)
                key = keys[at, cols]
                value = values[at, cols]
                heads = []
                for head in range(2):
                    query_h, key_h = head_operands(
                        upper, head, query, key, ones[...], mask[item]
                    )
                    probs = softmax_over_keys(nt(key_h, query_h))
                    heads.append(tn(probs.astype(BF16), value))
                attended[at, cols] = jnp.where(upper, heads[1], heads[0]).astype(BF16)
        place = pl.ds(pl.multiple_of(step * GROUP, GROUP), GROUP)
        total[...] += nn(attended[...], w_out[place, :])
        keep[1, :, place] = attended[...]

    @pl.when(step == FORWARD - 1)
    def _():
        summed = rows_out[...].astype(F32) + (total[...] + out_bias[...])
        unit, inv = norm(summed)
        result = unit * gain_one[...] + shift_one[...]
        scaled[...] = unit
        inverse[...] = inv
        normed[...] = result
        keep[2] = result.astype(BF16)
        total[...] = jnp.zeros_like(total)

    @pl.when((step >= FORWARD) & (step < BACKWARD))
    def _():
        chunk = step - FORWARD
        cols = pl.ds(pl.multiple_of(lax.rem(chunk, CHUNKS // 2) * CHUNK, CHUNK), CHUNK)
        ups = [nn(keep[2, at, :], w_up[...]) + up_bias[...] for at in parts]
        for at, upward in zip(parts, ups):
            active, steep = gelu_and_slope(upward)
            slope[chunk, at, :] = steep
            active = active.astype(BF16)

            @pl.when(chunk < CHUNKS // 2)
            def _(active=active, at=at):
                send[at, cols] = active

            @pl.when(chunk >= CHUNKS // 2)
            def _(active=active, at=at):
                act_mine[at, :] = active

            total[at, :] += nn(active, w_down[...])

    @pl.when(step == BACKWARD - 1)
    def _():
        unit, inv = norm(normed[...] + (total[...] + down_bias[...]))
        result = (unit * gain_two[...] + shift_two[...]).astype(BF16)
        cots = []
        for item in range(items):
            out_own[item] = result[item * span : item * span + SLOTS]
            out_other[item] = result[item * span + SLOTS : (item + 1) * span]
            cots += [cot_own[item], cot_other[item]]
        cot = jnp.concatenate(cots, axis=0).astype(F32)
        grad = norm_back(cot, unit, inv, gain_two[...])
        low = grad.astype(BF16)
        grad_second[...] = grad
        send[:, FF_HALF:] = low
        small[...] = jnp.zeros_like(small)
        small[3:4, :] = jnp.sum(low.astype(F32), axis=0, keepdims=True)
        small[4:5, :] = jnp.sum(cot * unit, axis=0, keepdims=True)
        small[5:6, :] = jnp.sum(cot, axis=0, keepdims=True)
        total[...] = grad

    @pl.when(step >= BACKWARD)
    def _():
        chunk = step - BACKWARD
        place = pl.multiple_of(half_chunk(chunk, pos) * CHUNK, CHUNK)
        downs = [nt(send[at, FF_HALF:], w_down[...]) for at in parts]
        sums = []
        for at, down in zip(parts, downs):
            low = (down * slope[chunk, at, :]).astype(BF16)

            @pl.when(chunk < CHUNKS // 2)
            def _(low=low, at=at):
                up_theirs[at, :] = low

            @pl.when(chunk >= CHUNKS // 2)
            def _(low=low, at=at):
                up_mine[at, :] = low

            sums.append(jnp.sum(low.astype(F32), axis=0, keepdims=True))
            total[at, :] += nt(low, w_up[...])
        up_bias_grad[:, pl.ds(place, CHUNK)] = sum(sums[1:], sums[0])

    @pl.when(step == STEPS - 1)
    def _():
        grad_normed = total[...]
        unit = scaled[...]
        grad = norm_back(grad_normed, unit, inverse[...], gain_one[...])
        grad_first[...] = grad
        branch[...] = grad.astype(BF16)
        mine = pl.multiple_of(pos[0] * HALF, HALF)
        theirs = pl.multiple_of((1 - pos[0]) * HALF, HALF)
        branch_mine[...] = branch[:, pl.ds(mine, HALF)]
        branch_theirs[...] = branch[:, pl.ds(theirs, HALF)]
        grad_attended[...] = nt(branch[...], w_out[...]).astype(BF16)
        small[0:1, :] = jnp.sum(branch[...].astype(F32), axis=0, keepdims=True)
        small[1:2, :] = jnp.sum(grad_normed * unit, axis=0, keepdims=True)
        small[2:3, :] = jnp.sum(grad_normed, axis=0, keepdims=True)


def half_chunk(j, pos):
    return lax.rem(j + (1 - pos[0]) * (CHUNKS // 2), CHUNKS)


def layer(
    pos,
    own,
    other,
    mask,
    ones,
    w_qkv,
    query_bias,
    value_bias,
    w_out,
    out_bias,
    gain_one,
    shift_one,
    w_up,
    up_bias,
    w_down,
    down_bias,
    gain_two,
    shift_two,
    cot_own,
    cot_other,
):
    items = own.shape[0]
    count = items * 2 * SLOTS
    half = CHUNKS // 2
    group = lambda j: jnp.minimum(j, GROUPS - 1)
    between = lambda j, first: jnp.clip(j - first, 0, half - 1)

    def chunk(j, pos):
        return half_chunk(
            jnp.where(j < BACKWARD, jnp.maximum(j - FORWARD, 0), j - BACKWARD), pos
        )

    row = pl.BlockSpec((1, GROUP), lambda j, pos: (0, group(j)))
    flat = pl.BlockSpec((count, GROUP), lambda j, pos: (0, group(j)))
    hidden = lambda first: pl.BlockSpec((count, CHUNK), lambda j, pos: (0, between(j, first)))
    weight = lambda k: pl.BlockSpec((WIDTH, GROUP), lambda j, pos: (0, k * GROUPS + group(j)))
    vector = whole((1, WIDTH))
    rows = whole(own.shape)
    shape = (count, WIDTH)
    full = whole(shape)
    narrow = whole((count, HALF))
    return run(
        functools.partial(layer_body, items),
        "layer",
        pos,
        (STEPS,),
        [
            (own, rows),
            (other, rows),
            (mask, whole(mask.shape)),
            (ones, whole(ones.shape)),
            (w_qkv, weight(0)),
            (w_qkv, weight(1)),
            (w_qkv, weight(2)),
            (query_bias, row),
            (value_bias, row),
            (w_out, whole((WIDTH, WIDTH))),
            (out_bias, vector),
            (gain_one, vector),
            (shift_one, vector),
            (w_up, pl.BlockSpec((WIDTH, CHUNK), lambda j, pos: (0, chunk(j, pos)))),
            (up_bias, pl.BlockSpec((1, CHUNK), lambda j, pos: (0, chunk(j, pos)))),
            (w_down, pl.BlockSpec((CHUNK, WIDTH), lambda j, pos: (chunk(j, pos), 0))),
            (down_bias, vector),
            (gain_two, vector),
            (shift_two, vector),
            (cot_own, rows),
            (cot_other, rows),
        ],
        [
            (shape, BF16, flat),
            (shape, BF16, flat),
            (shape, BF16, flat),
            ((3,) + shape, BF16, whole((3,) + shape)),
            ((count, FF_HALF), BF16, hidden(FORWARD + half)),
            ((count, FF_HALF + WIDTH), BF16, whole((count, FF_HALF + WIDTH))),
            (own.shape, BF16, rows),
            (own.shape, BF16, rows),
            ((count, FF_HALF), BF16, hidden(BACKWARD)),
            ((count, FF_HALF), BF16, hidden(BACKWARD + half)),
            ((1, FF), F32, whole((1, FF))),
            (shape, F32, full),
            ((count, HALF), BF16, narrow),
            ((count, HALF), BF16, narrow),
            (shape, BF16, full),
            ((8, WIDTH), F32, whole((8, WIDTH))),
        ],
        scratch=[
            pltpu.VMEM(shape, F32),
            pltpu.VMEM((count, GROUP), BF16),
            pltpu.VMEM((CHUNKS, count, CHUNK), F32),
            pltpu.VMEM(shape, F32),
            pltpu.VMEM(shape, F32),
            pltpu.VMEM((count, 1), F32),
            pltpu.VMEM(shape, F32),
            pltpu.VMEM(shape, BF16),
        ],
        us=30,
        mib=56,
    )


def keep_rows(which, count, cols, place):
    return pl.BlockSpec((None, count, cols), lambda j, pos: (which, 0, place(j, pos)))


def attend_back_half(
    items, mask, ones, queries, keys, values, grad_attended, w_q, w_k, w_v, joined
):
    span = 2 * SLOTS
    upper = lane_half((span, PAIR))
    for item in range(items):
        at = slice(item * span, (item + 1) * span)
        for pair in range(HALF // PAIR):
            cols = slice(pair * PAIR, (pair + 1) * PAIR)
            query = queries[at, cols] * jnp.asarray(SCALE, BF16)
            key = keys[at, cols]
            value = values[at, cols]
            grad_out = grad_attended[at, cols]
            none = jnp.zeros_like(grad_out)
            grads = []
            for head in range(2):
                query_h, key_h = head_operands(
                    upper, head, query, key, ones[...], mask[item]
                )
                probs = softmax_over_keys(nt(key_h, query_h))
                if head == 0:
                    grad_h = jnp.where(upper, none, grad_out)
                else:
                    grad_h = jnp.where(upper, grad_out, none)
                grad_probs = nt(value, grad_h)
                inner = jnp.sum(probs * grad_probs, axis=0, keepdims=True)
                grad_scores = (probs * (grad_probs - inner)).astype(BF16)
                grads.append(
                    (
                        tn(grad_scores, key) * SCALE,
                        nn(grad_scores, query),
                        nn(probs.astype(BF16), grad_out),
                    )
                )
            for index in range(3):
                place = slice(index * HALF + pair * PAIR, index * HALF + (pair + 1) * PAIR)
                joined[at, place] = jnp.where(
                    upper, grads[1][index], grads[0][index]
                ).astype(BF16)
    parts = [joined[:, index * HALF : (index + 1) * HALF] for index in range(3)]
    sums = [jnp.sum(parts[index].astype(F32), axis=0, keepdims=True) for index in (0, 2)]
    total = nt(parts[0], w_q[...]) + nt(parts[1], w_k[...]) + nt(parts[2], w_v[...])
    return total, sums


def attend_back_body(items, pos, *refs):
    *ins, first, second, grad_first, small_in, up_bias, theirs, mine, own, other, small, total, joined = refs
    step = pl.program_id(0)
    span = 2 * SLOTS
    part, sums = attend_back_half(items, *ins, joined)

    @pl.when(step == 0)
    def _():
        theirs[:, : 3 * HALF] = joined[...]
        theirs[:, 3 * HALF :] = first[...]
        total[...] = grad_first[...] + part
        small[...] = jnp.zeros_like(small)
        small[0:8, :] = small_in[...]
        for index in range(FF // WIDTH):
            small[6 + index : 7 + index, :] = up_bias[:, index * WIDTH : (index + 1) * WIDTH]

    @pl.when(step == 1)
    def _():
        mine[:, : 3 * HALF] = joined[...]
        mine[:, 3 * HALF :] = second[...]
        for item in range(items):
            at = slice(item * span, item * span + SLOTS)
            own[item] = total[at, :] + part[at]
            at = slice(item * span + SLOTS, (item + 1) * span)
            other[item] = (total[at, :] + part[at]).astype(BF16)

    place = pl.multiple_of(lax.rem(step + 1 + pos[0], 2) * HALF, HALF)
    for index in range(2):
        small[10 + index : 11 + index, pl.ds(place, HALF)] = sums[index]


def attend_back(
    pos, mask, ones, queries, keys, values, grad_attended, w_qkv, first, second, grad_first, small, up_bias, after
):
    count = queries.shape[0]
    items = mask.shape[0]
    half = lambda j, pos: lax.rem(j + 1 + pos[0], 2)
    flat = pl.BlockSpec((count, HALF), lambda j, pos: (0, half(j, pos)))
    weight = lambda k: pl.BlockSpec((WIDTH, HALF), lambda j, pos: (0, 2 * k + half(j, pos)))
    joined = ((count, 4 * HALF), BF16, whole((count, 4 * HALF)))
    rows = whole((items, SLOTS, WIDTH))
    return run(
        functools.partial(attend_back_body, items),
        "attend_back",
        pos,
        (2,),
        [
            (mask, whole(mask.shape)),
            (ones, whole(ones.shape)),
            (queries, flat),
            (keys, flat),
            (values, flat),
            (grad_attended, flat),
            (w_qkv, weight(0)),
            (w_qkv, weight(1)),
            (w_qkv, weight(2)),
        ]
        + [(a, whole(a.shape)) for a in (first, second, grad_first, small, up_bias)],
        [
            joined,
            joined,
            ((items, SLOTS, WIDTH), F32, rows),
            ((items, SLOTS, WIDTH), BF16, rows),
            ((16, WIDTH), F32, whole((16, WIDTH))),
        ],
        after=after,
        scratch=[pltpu.VMEM((count, WIDTH), F32), pltpu.VMEM((count, 3 * HALF), BF16)],
        us=12,
        mib=32,
    )


TALL = HALF
LOW = TALL // 2
FAR, ACROSS, ALONG, OWN = 3, 2, 1, 0
PIECE = (TALL, WIDTH)


def quarter(pos, there):
    return pos[1] ^ (there >> 1), pos[2] ^ (there & 1)


def order_of(kind, step):
    first, second = (ACROSS, ALONG) if kind == "up" else (ALONG, ACROSS)
    return jnp.where(step == 0, FAR, jnp.where(step == 1, first, jnp.where(step == 2, second, OWN)))


def gradient_body(kind, block, outs, pos, *refs):
    ins, outs = refs[:-outs], refs[-outs:]
    step = pl.program_id(0)
    value = block(quarter(pos, order_of(kind, step))[1], *ins).astype(BF16)
    if kind == "mixed":
        targets = [None, outs[2], outs[3], outs[4]]
    else:
        targets = [outs[0].at[0], outs[0].at[1], outs[1], outs[2]]
    for index, target in enumerate(targets):

        @pl.when(step == index)
        def _(target=target):
            if target is None:
                outs[0][...] = value[:LOW]
                outs[1][...] = value[LOW:]
            else:
                target[...] = value


def plain_block(along, left_a, left_b, right_a, right_b):
    return tn(left_a[...], right_a[...]) + tn(left_b[...], right_b[...])


def mixed_block(along, rows_a, rows_b, att_a, att_b, right_a, right_b):
    left_a = jnp.where(along == 0, rows_a[...], att_a[...])
    left_b = jnp.where(along == 0, rows_b[...], att_b[...])
    return jnp.concatenate(
        [
            tn(rows_a[...], right_a[:, :HALF]) + tn(rows_b[...], right_b[:, :HALF]),
            tn(left_a, right_a[:, HALF:]) + tn(left_b, right_b[:, HALF:]),
        ],
        axis=1,
    )


def gradient(kind, pos, operands, after):
    count = operands[-1].shape[0]
    across = lambda j, pos: quarter(pos, order_of(kind, j))[0]
    along = lambda j, pos: quarter(pos, order_of(kind, j))[1]
    block = plain_block
    if kind == "down":
        lefts = pl.BlockSpec(
            (count, TALL), lambda j, pos: (0, 2 * across(j, pos) + along(j, pos))
        )
        rights = pl.BlockSpec((count, WIDTH), lambda j, pos: (0, FF_HALF // WIDTH))
        specs = [lefts, lefts, rights, rights]
    else:
        rights = pl.BlockSpec((count, WIDTH), lambda j, pos: (0, along(j, pos)))
        if kind == "up":
            lefts = keep_rows(2, count, TALL, across)
            specs = [lefts, lefts, rights, rights]
        else:
            rows, att = keep_rows(0, count, TALL, across), keep_rows(1, count, TALL, across)
            specs = [rows, rows, att, att, rights, rights]
            block = mixed_block
    if kind == "mixed":
        shapes = [(LOW, WIDTH)] * 2 + [PIECE] * 3
    else:
        shapes = [(2,) + PIECE] + [PIECE] * 2
    return run(
        functools.partial(gradient_body, kind, block, len(shapes)),
        kind + "_gradient",
        pos,
        (4,),
        list(zip(operands, specs)),
        [(shape, BF16, whole(shape)) for shape in shapes],
        after=after,
        us=5,
        mib=20,
    )


def sum_body(share, pos, *refs):
    ins = refs[:-3] if share else refs[:-1]
    total = ins[0][...].astype(F32)
    for ref in ins[1:]:
        total = total + ref[...].astype(F32)
    if not share:
        refs[-1][...] = total.astype(BF16)
        return
    held = refs[-1]
    held[...] = total
    for turn in range(2):
        first = pl.multiple_of((pos[3] ^ turn) * LOW, LOW)
        refs[turn - 3][...] = held[pl.ds(first, LOW), :].astype(BF16)


def sum_of(pos, arrays, after, share=False, carry=(), us=1):
    shape = arrays[0].shape
    item = lambda index: pl.BlockSpec((None,) + PIECE, lambda *_: (index, 0, 0))
    shapes = [(LOW, WIDTH)] * 2 if share else [shape]
    out, *more = run(
        functools.partial(sum_body, share),
        "sum_shares" if share else "sum_of",
        pos,
        (1,),
        [
            (a[0], item(a[1])) if isinstance(a, tuple) else (a, whole(shape))
            for a in arrays
        ],
        [(shape, BF16, whole(shape)) for shape in shapes],
        after=after,
        scratch=[pltpu.VMEM(shape, F32)] if share else [],
        us=us,
        mib=8,
        carry=carry,
    )
    return (out if share else out[0]), *more


def sides_body(pos, along, across, low, high, along_out, across_out):
    along_out[:LOW, :] = along[:LOW, :]
    along_out[LOW:, :] = (along[LOW:, :].astype(F32) + high[...].astype(F32)).astype(BF16)
    across_out[:LOW, :] = (across[:LOW, :].astype(F32) + low[...].astype(F32)).astype(BF16)
    across_out[LOW:, :] = across[LOW:, :]


def sum_sides(pos, along, across, low, high, after, carry=()):
    return run(
        sides_body,
        "sum_sides",
        pos,
        (1,),
        [(a, whole(a.shape)) for a in (along, across, low, high)],
        [(PIECE, BF16, whole(PIECE))] * 2,
        after=after,
        carry=carry,
        us=0.1,
        mib=8,
    )


def split_body(pos, own, first, second, low, high, packed):
    low[...] = first[:LOW, :]
    high[...] = second[LOW:, :]
    for index, ref in enumerate((own, first, second)):
        packed[index] = ref[...]


def split(pos, own, first, second, after):
    half = (LOW, WIDTH)
    return run(
        split_body,
        "split",
        pos,
        (1,),
        [(a, whole(PIECE)) for a in (own, first, second)],
        [(half, BF16, whole(half))] * 2 + [((3,) + PIECE, BF16, whole((3,) + PIECE))],
        after=after,
        us=1,
        mib=10,
    )


def pack_body(pos, *refs):
    for index, ref in enumerate(refs[:-1]):
        refs[-1][index] = ref[...]


def pack(pos, pieces, after):
    shape = (len(pieces),) + PIECE
    out, token = run(
        pack_body,
        "pack",
        pos,
        (1,),
        [(a, whole(PIECE)) for a in pieces],
        [(shape, BF16, whole(shape))],
        after=after,
        us=0.1,
        mib=12,
    )
    return out[0], token


def stack_halves(pos, low, high, after):
    half = (LOW, WIDTH)
    out, token = run(
        pack_body,
        "stack_halves",
        pos,
        (1,),
        [(low, whole(half)), (high, whole(half))],
        [((2,) + half, BF16, whole((2,) + half))],
        after=after,
        us=0.1,
        mib=6,
    )
    return out[0], token


def join_body(pos, mine, theirs, out):
    for turn, ref in enumerate((mine, theirs)):
        first = pl.multiple_of((pos[3] ^ turn) * LOW, LOW)
        out[pl.ds(first, LOW), :] = ref[...]


def join_shares(pos, shares, after, carry=()):
    out, *more = run(
        join_body,
        "join_shares",
        pos,
        (1,),
        [(a, whole(a.shape)) for a in shares],
        [(PIECE, BF16, whole(PIECE))],
        after=after,
        us=0.1,
        mib=6,
        carry=carry,
    )
    return out[0], *more


def place_body(kind, entries, outs, pos, *refs):
    sources = iter(refs)
    pieces = []
    for _, _, _, _, index in entries:
        if not index:
            ref = next(sources)
        pieces.append(ref if index is None else ref.at[index])
    targets = refs[len(refs) - 4 - outs : len(refs) - 4]
    taken, given, in_sems, out_sems = refs[-4:]
    fetches = []
    for index, (rows, *_) in enumerate(entries):
        fetch = pltpu.make_async_copy(
            pieces[index], taken.at[index, pl.ds(0, rows)], in_sems.at[index]
        )
        fetch.start()
        fetches.append(fetch)

    def sends(index):
        rows, theirs, there, start, _ = entries[index]
        half = pos[0] ^ theirs
        across, along = quarter(pos, there)
        source = given.at[index]
        if kind == "down":
            first = pl.multiple_of((4 * half + 2 * across + along) * TALL + start, LOW)
            yield None, source.at[pl.ds(0, rows)], targets[0].at[pl.ds(first, rows)], 0
            return
        first = pl.multiple_of(across * TALL + start, LOW)
        if kind == "up":
            column = pl.multiple_of((2 * half + along) * WIDTH, WIDTH)
            target = targets[0].at[pl.ds(first, rows), pl.ds(column, WIDTH)]
            yield None, source.at[pl.ds(0, rows)], target, 0
            return
        for part in range(2):
            source_part = source.at[pl.ds(0, rows), pl.ds(part * HALF, HALF)]
            column = pl.multiple_of(jnp.minimum(2 * along + part, 2) * WIDTH + half * HALF, HALF)
            target = targets[0].at[pl.ds(first, rows), pl.ds(column, HALF)]
            if part == 0:
                yield None, source_part, target, 0
            else:
                yield along == 0, source_part, target, 1
                column = pl.multiple_of(half * HALF, HALF)
                target = targets[1].at[pl.ds(first, rows), pl.ds(column, HALF)]
                yield along == 1, source_part, target, 1

    def each(index, act):
        for condition, source, target, sem in sends(index):
            copy = pltpu.make_async_copy(source, target, out_sems.at[index, sem])
            if condition is None:
                act(copy)
            else:

                @pl.when(condition)
                def _(copy=copy):
                    act(copy)

    for index, (rows, *_) in enumerate(entries):
        fetches[index].wait()
        given[index, :rows, :] = taken[index, :rows, :].astype(F32)
        each(index, lambda copy: copy.start())
    for index in range(len(entries)):
        each(index, lambda copy: copy.wait())


def place(kind, pos, pieces, before, after):
    pieces = [piece if len(piece) == 5 else piece + (None,) for piece in pieces]
    entries = tuple((p.shape[-2],) + tuple(more) for p, *more in pieces)
    shapes = {
        "down": [(FF, WIDTH)],
        "up": [(WIDTH, FF)],
        "mixed": [(WIDTH, 3 * WIDTH), (WIDTH, WIDTH)],
    }[kind]
    anywhere = pl.BlockSpec(memory_space=pl.ANY)
    arrays = [p for p, *_, index in pieces if not index]
    ins = [(a, anywhere) for a in arrays + list(before)]
    count = len(entries)
    return run(
        functools.partial(place_body, kind, entries, len(shapes)),
        "place_" + kind,
        pos,
        (1,),
        ins,
        [(shape, F32, anywhere) for shape in shapes],
        after=after,
        scratch=[
            pltpu.VMEM((count, TALL, WIDTH), BF16),
            pltpu.VMEM((count, TALL, WIDTH), F32),
            pltpu.SemaphoreType.DMA((count,)),
            pltpu.SemaphoreType.DMA((count, 2)),
        ],
        aliases={1 + len(arrays) + index: index for index in range(len(before))},
        us=0.02,
        mib=22,
    )


def place_rows_body(pos, own, got, own_grad, got_grad, out, grad):
    @pl.when(pl.program_id(0) == 0)
    def _():
        out[...] = own[...]
        grad[...] = own_grad[...]

    @pl.when(pl.program_id(0) == 1)
    def _():
        out[...] = got[...]
        grad[...] = got_grad[...].astype(F32)


def place_rows(pos, own, got, own_grad, got_grad, after):
    items = own.shape[0]
    spec = pl.BlockSpec(own.shape, lambda step, pos: (pos[1] ^ step, 0, 0))
    shape = (2 * items,) + own.shape[1:]
    return run(
        place_rows_body,
        "place_rows",
        pos,
        (2,),
        [(a, whole(own.shape)) for a in (own, got, own_grad, got_grad)],
        [(shape, BF16, spec), (shape, F32, spec)],
        after=after,
        us=0.02,
        mib=10,
    )


def local(
    batch,
    tokens,
    caption_lengths,
    region_mask,
    w_qkv,
    query_bias,
    value_bias,
    w_out,
    out_bias,
    w_up,
    up_bias,
    w_down,
    down_bias,
    gain_one,
    shift_one,
    gain_two,
    shift_two,
    cotangent,
):
    swap_core = [(i, i ^ 1) for i in range(batch)]
    swap_along = [(i, i ^ 2) for i in range(batch)]
    swap_across = [(0, 1), (1, 0)]
    line = [[4 * k + i for k in range(batch // 4)] for i in range(4)]
    same_core = [[2 * k + i for k in range(batch // 2)] for i in range(2)]
    core = lambda a: lax.ppermute(a, "batch", swap_core)
    along = lambda a: lax.ppermute(a, "batch", swap_along)
    across = lambda a: lax.ppermute(a, "mod", swap_across)

    place_y = lax.axis_index("mod")
    place_b = lax.axis_index("batch")
    pos = jnp.stack([place_b % 2, place_y, (place_b // 2) % 2, (place_b // 4) % 2]).astype(jnp.int32)
    items = tokens.shape[0] // 2
    mine = place_y * items
    rest = (1 - place_y) * items
    rows = lambda a, start: lax.dynamic_slice_in_dim(a, start, items, axis=0)

    other_tokens = across(rows(tokens, rest))
    other_cot = across(rows(cotangent, rest))
    own_tokens = rows(tokens, mine)
    own_cot = rows(cotangent, mine)

    slot = lax.broadcasted_iota(jnp.int32, (items, SLOTS), 1)
    text = slot < rows(caption_lengths, mine)[:, None]
    region = rows(region_mask, mine) > 0
    valid = jnp.concatenate(
        [jnp.where(place_y == 0, text, region), jnp.where(place_y == 0, region, text)], axis=1
    )
    lane = lax.broadcasted_iota(jnp.int32, (1, 1, PAIR), 2) % HEAD_DIM == 0
    mask = jnp.where(lane & ~valid[:, :, None], MASKED, 0.0).astype(BF16)
    ones = jnp.where(
        lax.broadcasted_iota(jnp.int32, (2 * SLOTS, PAIR), 1) % HEAD_DIM == 0, 1.0, 0.0
    ).astype(BF16)
    line_of = lambda a: a.reshape(1, -1)

    (
        (
            queries,
            keys,
            values,
            keep,
            act_mine,
            send,
            out_own,
            out_other,
            up_theirs,
            up_mine,
            up_bias_grad,
            grad_first,
            branch_theirs,
            branch_mine,
            grad_attended,
            small,
        ),
        done,
    ) = layer(
        pos,
        own_tokens,
        other_tokens,
        mask,
        ones,
        w_qkv,
        line_of(query_bias),
        line_of(value_bias),
        w_out,
        line_of(out_bias),
        line_of(gain_one),
        line_of(shift_one),
        w_up,
        line_of(up_bias),
        w_down,
        line_of(down_bias),
        line_of(gain_two),
        line_of(shift_two),
        own_cot,
        other_cot,
    )
    send_got, keep_got, up_got = core(send), core(keep), core(up_theirs)
    out_got = across(out_other)
    by_shares = batch == 16
    near = lambda a: lax.ppermute(a, "batch", [(i, i ^ 4) for i in range(batch)])
    wide = lambda a: lax.ppermute(a, "batch", [(i, i ^ 8) for i in range(batch)])

    def line_sum(piece, turn):
        return lax.psum(piece, "batch", axis_index_groups=line[turn:] + line[:turn])

    hops = [across]
    bit = 2
    while bit < batch:
        hops.append(
            lambda a, bit=bit: lax.ppermute(a, "batch", [(i, i ^ bit) for i in range(batch)])
        )
        bit *= 2
    hops.append(core)

    def ride(kernel, *args, **more):
        nonlocal small, got, riding
        if not riding:
            return kernel(*args, **more)
        out, done, small = kernel(
            *args, **more, carry=(small,) if got is None else (small, got)
        )
        got = hops.pop(0)(small) if hops else None
        return out, done

    (down_pair, down_across, down_own), done = gradient(
        "down", pos, (act_mine, send_got, send, send_got), (done,)
    )
    down_pair = along(down_pair)
    (up_pair, up_along, up_own), done = gradient(
        "up", pos, (keep, keep_got, up_mine, up_got), (done, out_got)
    )
    up_pair = across(up_pair)
    (joint_theirs, joint_mine, grad_own, grad_other, small), done = attend_back(
        pos,
        mask,
        ones,
        queries,
        keys,
        values,
        grad_attended,
        w_qkv,
        branch_theirs,
        branch_mine,
        grad_first,
        small,
        up_bias_grad,
        (done,),
    )
    joint_got = core(joint_theirs)
    down_across, done = sum_of(pos, (down_across, (down_pair, 0)), (done,))
    down_across = across(down_across)
    up_along, done = sum_of(pos, (up_along, (up_pair, 0)), (done,))
    up_along = along(up_along)
    (mixed_low, mixed_high, mixed_along, mixed_across, mixed_own), done = gradient(
        "mixed", pos, (keep, keep_got, keep, keep_got, joint_mine, joint_got), (done,)
    )
    mixed_low, mixed_high = along(mixed_low), across(mixed_high)
    got, riding = None, False

    def halves(arrays, done, turn):
        parts, done = ride(sum_of, pos, arrays, (done,), share=by_shares, us=0.1)
        if by_shares:
            return (parts[0], near(parts[1])), done
        return line_sum(parts, turn), done

    def widen(parts, after):
        if not by_shares:
            return parts, after[0]
        half, done = ride(sum_of, pos, parts, after, us=0.1)
        return (half, wide(half)), done

    def narrow(parts, after):
        if not by_shares:
            return parts, after[0]
        half, done = ride(sum_of, pos, parts, after, us=0.1)
        return (half, near(half)), done

    def joined(parts, after):
        return ride(join_shares, pos, parts, after) if by_shares else (parts, after[0])

    down_sum, done = halves((down_own, (down_pair, 1), down_across), done, 0)
    up_sum, done = halves((up_own, (up_pair, 1), up_along), done, 1)
    (mixed_along, mixed_across), done = ride(
        sum_sides, pos, mixed_along, mixed_across, mixed_low, mixed_high, (done,)
    )
    mixed_along, mixed_across = along(mixed_along), across(mixed_across)
    down_sum, done = widen(down_sum, (done,))
    riding = True
    down_sum, done = narrow(down_sum, (done,))
    up_sum, done = widen(up_sum, (done,))
    mixed_sum, done = halves((mixed_own, mixed_along, mixed_across), done, 2)
    grad_got = across(grad_other)
    down_sum, done = joined(down_sum, (done, grad_got))
    down_x, down_y = along(down_sum), across(down_sum)
    up_sum, done = narrow(up_sum, (done,))
    mixed_sum, done = widen(mixed_sum, (done, down_x, down_y))
    up_sum, done = joined(up_sum, (done,))
    up_x, up_y = along(up_sum), across(up_sum)
    mixed_sum, done = narrow(mixed_sum, (done, up_x, up_y))
    while hops or got is not None:
        small = small + (hops.pop(0)(small) if got is None else got)
        got = None
    vectors = [small[index] for index in range(12)]
    vectors[6] = small[6:10].reshape(FF)
    seen = tuple(vectors[index] for index in (0, 1, 2, 3, 4, 5, 6, 10, 11))
    down_pack, done = pack(pos, (down_sum, down_x, down_y, across(down_x)), (done,))
    mixed_sum, done = joined(mixed_sum, (done,))
    mixed_x, mixed_y = along(mixed_sum), across(mixed_sum)
    up_pack, done = pack(pos, (up_sum, up_x, up_y, along(up_y)), (done,))
    (layer_output, input_grad), done = place_rows(
        pos, out_own, out_got, grad_own, grad_got, (done,)
    )
    def both(pieces):
        return [(p, 0, there, start) for p, there, start in pieces] + [
            (core(p), 1, there, start) for p, there, start in pieces
        ]

    def packed(pieces):
        places = list(enumerate((OWN, ALONG, ACROSS, FAR)))[: pieces.shape[0]]
        return [
            (array, theirs, there, 0, index)
            for theirs, array in enumerate((pieces, core(pieces)))
            for index, there in places
        ]

    (grad_down,), done = place(
        "down",
        pos,
        packed(down_pack),
        (),
        (done,),
    )
    (grad_up,), done = place(
        "up",
        pos,
        packed(up_pack),
        (),
        (done,),
    )
    (mixed_low, mixed_high, mixed_pack), done = split(pos, mixed_sum, mixed_x, mixed_y, (done,))
    mixed_low, mixed_high = across(mixed_low), along(mixed_high)
    partial, done = place(
        "mixed",
        pos,
        packed(mixed_pack),
        (),
        (done,),
    )
    last, done = stack_halves(pos, mixed_low, mixed_high, (done,) + seen)
    ends = [
        (array, theirs, FAR, start, index)
        for theirs, array in enumerate((last, core(last)))
        for index, start in enumerate((0, LOW))
    ]
    (grad_qkv, grad_out), done = place("mixed", pos, ends, partial, (done,))
    return (
        layer_output,
        input_grad,
        grad_qkv,
        vectors[10],
        vectors[11],
        grad_out,
        vectors[0],
        grad_up,
        vectors[6],
        grad_down,
        vectors[3],
        vectors[1],
        vectors[2],
        vectors[4],
        vectors[5],
    )


def solution(mesh):
    rows = P("batch", "mod", None)
    return jax.shard_map(
        functools.partial(local, mesh.shape["batch"]),
        mesh=mesh,
        in_specs=(rows, P("batch"), P("batch", None)) + (P(),) * 13 + (rows,),
        out_specs=(rows, rows) + (P(),) * 13,
        check_vma=False,
    )
```

time: 960 us -> 255 us (0.27)
  blocking collectives: 496 us -> 0 us
  waiting for transfers between devices: 208 us -> 68.8 us
  Pallas kernels: 0 us -> 112 us
  local copies, waits for them, and re-layouts: 122 us -> 16.9 us
  matrix products: 88.5 us -> 0 us
  starting transfers between devices: 0.33 us -> 52.6 us
  other arithmetic: 21 us -> 2.14 us
  between operations: 15.1 us -> 1.56 us
    unnamed x2 -> x0, blocking collectives: 496 us -> none
    all_gather x6 -> x0, waiting for transfers between devices: 208 us -> none  [the longest x1 57.9 us: local(): lax.all_gather(share_up.astype(jnp.bfloat16), ('mod', 'batch'), axis=0, t...]
    pallas_call x0 -> x29, Pallas kernels: none -> 112 us  [run(): pl.pallas_call(wrapped, grid_spec=pltpu.PrefetchScalarGridSpec(num_scalar...]
    dot_general x18 -> x0, matrix products: 88.5 us -> none  [the longest x4 26.2 us: multiply(): return jnp.dot(left, right, preferred_element_type=jnp.float32)]
    ppermute x0 -> x44, waiting for transfers between devices: none -> 68.8 us  [the longest x14 38.1 us: local(): across = lambda a: lax.ppermute(a, 'mod', swap_across)]
    reshape x10 -> x9, local copies, waits for them, and re-layouts: 58.4 us -> 5.37 us  [the longest x8 4.65 us: local(): line_of = lambda a: a.reshape(1, -1)]
    ppermute x0 -> x44, starting transfers between devices: none -> 52.6 us  [the longest x14 19.7 us: local(): across = lambda a: lax.ppermute(a, 'mod', swap_across)]
    unnamed x96 -> x90, local copies, waits for them, and re-layouts: 24.8 us -> 5.99 us
  transfers between devices with their start and end apart: 8 -> 44, of which waited for: 5 -> 21; matrix products, arithmetic and copies ran while one was open for 13% -> 4% of each run, Pallas kernels for 0% -> 25%
where the time goes in v1:
time: 255 us; the launch traced here: 254 us
  Pallas kernels  112 us (44%)
  waiting for transfers between devices  68.8 us (27%)
  starting transfers between devices  52.6 us (21%)
  local copies, waits for them, and re-layouts  16.9 us (7%)
    pallas_call x29, Pallas kernels, run(): pl.pallas_call(wrapped, grid_spec=pltpu.PrefetchScalarGridSpec(num_scalar...  112 us
    ppermute x14, waiting for transfers between devices, local(): across = lambda a: lax.ppermute(a, 'mod', swap_across)  38.1 us
    ppermute x14, starting transfers between devices, local(): across = lambda a: lax.ppermute(a, 'mod', swap_across)  19.7 us
    ppermute x6, starting transfers between devices, local(): lax.ppermute(a, 'batch', [(i, i ^ 4) for i in range(batch)])  10.2 us
    ppermute x9, starting transfers between devices, local(): along = lambda a: lax.ppermute(a, 'batch', swap_along)  9.93 us
    ppermute x9, waiting for transfers between devices, local(): along = lambda a: lax.ppermute(a, 'batch', swap_along)  9.43 us
    ppermute x3, waiting for transfers between devices, local(): lax.ppermute(a, 'batch', [(i, i ^ 8) for i in range(batch)])  8.01 us
    unnamed x90, local copies, waits for them, and re-layouts  5.99 us
  transfers between devices with their start and end apart: 44, of which 21 were waited for; matrix products, arithmetic and copies ran while one was open for 4% of the time, Pallas kernels for 25%

profile of v1, /device:TPU:0, one launch (start us, length us, event | category | flops | bytes accessed | tf_op | source)
XLA Modules:
  0.0 254.1 jit_solution(10282590068366139021)
XLA Ops:
  0.8 2.0 constant_dynamic-slice_fusion.3
  2.7 3.0 %collective-permute-start = (bf16[2,128,768]{2,1,0:T(8,128)(2,1)S(1)}, bf16[2,128,768]{2,1,0:T(8,128)(2,1)S(1)}, u32[]{:S(2)}, u32[]{:S(2)}) collective-permute-start(bf16[2,128,768]{2,1,0:T(8,128)(2,1)S(1)} %get-tuple-element.227), channel_id=1, source_target_pairs={{0,16},{16,0},{1,17},{17,1},{2,18},{18,2},{3,19},{19,3},{4,20},{20... | collective-permute-start | bytes 1179656 | tf_op jit(solution)/shard_map/ppermute | solution.py:936
  15.6 7.6 %collective-permute-done.1.refs_21_ = bf16[2,128,768]{2,1,0:T(8,128)(2,1)S(1)} collective-permute-done((bf16[2,128,768]{2,1,0:T(8,128)(2,1)S(1)}, bf16[2,128,768]{2,1,0:T(8,128)(2,1)S(1)}, u32[]{:S(2)}, u32[]{:S(2)}) %collective-permute-start.1) | collective-permute-done | bytes 393248 | tf_op jit(solution)/shard_map/ppermute | solution.py:936
  24.0 42.6 %layer.1 = (bf16[512,768]{1,0:T(8,128)(2,1)}, bf16[512,768]{1,0:T(8,128)(2,1)}, bf16[512,768]{1,0:T(8,128)(2,1)}, bf16[3,512,768]{2,1,0:T(8,128)(2,1)}, bf16[512...) custom-call(s32[4]{0:T(128)} %pad_add_fusion.refs_0_, ...), custom_call_target="tpu_custom_call" | custom-call | flops 299999985664 | bytes 1000 | tf_op jit(solution)/shard_map/layer/pallas_call | solution.py:68
  69.0 2.4 collective-permute-done.5.refs_2_.refs_4_
  75.2 5.8 %down_gradient.1 = (bf16[2,384,768]{2,1,0:T(8,128)(2,1)}, bf16[384,768]{1,0:T(8,128)(2,1)S(1)}, bf16[384,768]{1,0:T(8,128)(2,1)S(1)}, f32[8,128]{1,0:T(8,128)S(1)}) custom-call(s32[4]{0:T(128)S(1)} %copy-done.6, bf16[512,1536]{1,0:T(8,128)(2,1)S(1)} %copy-done.21, bf16[512,2304]{1,0:T(8,128)(2,1)S(1)} %collective-permute-done.5.refs_2_.refs_4_, ...), custom_call_target="tpu_custom_call" | custom-call | flops 49999998976 | bytes 1000 | tf_op jit(solution)/shard_map/down_gradient/pallas_call | solution.py:68
  82.9 4.9 %up_gradient.1 = (bf16[2,384,768]{2,1,0:T(8,128)(2,1)S(1)}, bf16[384,768]{1,0:T(8,128)(2,1)S(1)}, bf16[384,768]{1,0:T(8,128)(2,1)S(1)}, f32[8,128]{1,0:T(8,128)S(1)}) custom-call(s32[4]{0:T(128)S(1)} %copy-done.6, bf16[3,512,768]{2,1,0:T(8,128)(2,1)S(1)} %copy-done.19, bf16[3,512,768]{2,1,0:T(8,128)(2,1)S(1)} %collective-permute-done.3.refs_2_.refs_4_, ...), custom_call_target="tpu_custom_call" | custom-call | flops 49999998976 | bytes 1000 | tf_op jit(solution)/shard_map/up_gradient/pallas_call | solution.py:68
  89.4 14.6 %attend_back.1 = (bf16[512,1536]{1,0:T(8,128)(2,1)S(1)}, bf16[512,1536]{1,0:T(8,128)(2,1)S(1)}, f32[2,128,768]{2,1,0:T(8,128)S(1)}, bf16[2,128,768]{2,1,0:T(8,12...) custom-call(s32[4]{0:T(128)S(1)} %copy-done.6, bf16[2,256,128]{2,1,0:T(8,128)(2,1)S(1)} %copy-done.3, ...), custom_call_target="tpu_custom_call" | custom-call | flops 120000004096 | bytes 1000 | tf_op jit(solution)/shard_map/attend_back/pallas_call | solution.py:68
  104.2 5.2 %collective-permute-done.8.refs_2_ = bf16[2,384,768]{2,1,0:T(8,128)(2,1)} collective-permute-done((bf16[2,384,768]{2,1,0:T(8,128)(2,1)}, bf16[2,384,768]{2,1,0:T(8,128)(2,1)}, u32[]{:S(2)}, u32[]{:S(2)}) %collective-permute-start.8) | collective-permute-done | bytes 1179680 | tf_op jit(solution)/shard_map/ppermute | solution.py:935
  112.9 3.7 %collective-permute-done.7.refs_2_ = bf16[2,384,768]{2,1,0:T(8,128)(2,1)S(1)} collective-permute-done((bf16[2,384,768]{2,1,0:T(8,128)(2,1)S(1)}, bf16[2,384,768]{2,1,0:T(8,128)(2,1)S(1)}, u32[]{:S(2)}, u32[]{:S(2)}) %collective-permute-start.7) | collective-permute-done | bytes 1179680 | tf_op jit(solution)/shard_map/ppermute | solution.py:936
  117.6 6.2 %mixed_gradient.1 = (bf16[192,768]{1,0:T(8,128)(2,1)S(1)}, bf16[192,768]{1,0:T(8,128)(2,1)S(1)}, bf16[384,768]{1,0:T(8,128)(2,1)S(1)}, bf16[384,768]{1,0:T(8,128...) custom-call(s32[4]{0:T(128)S(1)} %copy-done.6, bf16[3,512,768]{2,1,0:T(8,128)(2,1)S(1)} %copy-done.19, ...), custom_call_target="tpu_custom_call" | custom-call | flops 49999998976 | bytes 1000 | tf_op jit(solution)/shard_map/mixed_gradient/pallas_call | solution.py:68
  127.3 2.1 collective-permute-done.10.refs_3_
  129.3 2.0 sum_shares.3
  134.6 2.2 collective-permute-done.14.refs_3_
  140.3 2.6 %collective-permute-start.16 = (bf16[192,768]{1,0:T(8,128)(2,1)S(1)}, bf16[192,768]{1,0:T(8,128)(2,1)S(1)}, u32[]{:S(2)}, u32[]{:S(2)}) collective-permute-start(bf16[192,768]{1,0:T(8,128)(2,1)S(1)} %get-tuple-element.162.refs_1_), channel_id=1, source_target_pairs={{0,8},{1,9},{2,10},{3,11},{4,12},{5,13},{6,14},{7,15},{8,0},{9,1},... | collective-permute-start | bytes 884744 | tf_op jit(solution)/shard_map/ppermute | solution.py:1010
  145.0 8.0 %collective-permute-done.16.refs_2_ = bf16[192,768]{1,0:T(8,128)(2,1)S(1)} collective-permute-done((bf16[192,768]{1,0:T(8,128)(2,1)S(1)}, bf16[192,768]{1,0:T(8,128)(2,1)S(1)}, u32[]{:S(2)}, u32[]{:S(2)}) %collective-permute-start.16) | collective-permute-done | bytes 294944 | tf_op jit(solution)/shard_map/ppermute | solution.py:1010
  154.8 4.6 %collective-permute-done.17.refs_5_ = f32[16,768]{1,0:T(8,128)S(1)} collective-permute-done((f32[16,768]{1,0:T(8,128)S(1)}, f32[16,768]{1,0:T(8,128)S(1)}, u32[]{:S(2)}, u32[]{:S(2)}) %collective-permute-start.17) | collective-permute-done | bytes 49184 | tf_op jit(solution)/shard_map/ppermute | solution.py:936
  161.7 2.5 collective-permute-done.22.refs_6_
  166.9 2.6 %collective-permute-start.18 = (bf16[192,768]{1,0:T(8,128)(2,1)S(1)}, bf16[192,768]{1,0:T(8,128)(2,1)S(1)}, u32[]{:S(2)}, u32[]{:S(2)}) collective-permute-start(bf16[192,768]{1,0:T(8,128)(2,1)S(1)} %get-tuple-element.167.refs_1_), channel_id=1, source_target_pairs={{0,8},{1,9},{2,10},{3,11},{4,12},{5,13},{6,14},{7,15},{8,0},{9,1},... | collective-permute-start | bytes 884744 | tf_op jit(solution)/shard_map/ppermute | solution.py:1010
  171.9 2.8 %collective-permute-start.28 = (bf16[384,768]{1,0:T(8,128)(2,1)S(1)}, bf16[384,768]{1,0:T(8,128)(2,1)S(1)}, u32[]{:S(2)}, u32[]{:S(2)}) collective-permute-start(bf16[384,768]{1,0:T(8,128)(2,1)S(1)} %get-tuple-element.182.refs_1_), channel_id=1, source_target_pairs={{0,16},{16,0},{1,17},{17,1},{2,18},{18,2},{3,19},{19,3},{4,20},{20... | collective-permute-start | bytes 1769480 | tf_op jit(solution)/shard_map/ppermute | solution.py:936
  176.3 2.1 collective-permute-start.24
  178.4 3.0 %collective-permute-start.26 = (bf16[192,768]{1,0:T(8,128)(2,1)S(1)}, bf16[192,768]{1,0:T(8,128)(2,1)S(1)}, u32[]{:S(2)}, u32[]{:S(2)}) collective-permute-start(bf16[192,768]{1,0:T(8,128)(2,1)S(1)} %get-tuple-element.180), channel_id=1, source_target_pairs={{0,4},{1,5},{2,6},{3,7},{4,0},{5,1},{6,2},{7,3},{8,12},{9,13},{10,... | collective-permute-start | bytes 884744 | tf_op jit(solution)/shard_map/ppermute | solution.py:1009
  182.0 2.7 %collective-permute-start.25 = (bf16[192,768]{1,0:T(8,128)(2,1)S(1)}, bf16[192,768]{1,0:T(8,128)(2,1)S(1)}, u32[]{:S(2)}, u32[]{:S(2)}) collective-permute-start(bf16[192,768]{1,0:T(8,128)(2,1)S(1)} %get-tuple-element.178.refs_1_), channel_id=1, source_target_pairs={{0,4},{1,5},{2,6},{3,7},{4,0},{5,1},{6,2},{7,3},{8,12},{9,13},{10,... | collective-permute-start | bytes 884744 | tf_op jit(solution)/shard_map/ppermute | solution.py:1009
  187.4 2.5 collective-permute-done.25.refs_2_
  195.1 11.8 %collective-permute-done.31.refs_5_.refs_3_ = bf16[384,768]{1,0:T(8,128)(2,1)S(1)} collective-permute-done((bf16[384,768]{1,0:T(8,128)(2,1)S(1)}, bf16[384,768]{1,0:T(8,128)(2,1)S(1)}, u32[]{:S(2)}, u32[]{:S(2)}) %collective-permute-start.31) | collective-permute-done | bytes 589856 | tf_op jit(solution)/shard_map/ppermute | solution.py:936
  209.5 5.8 %collective-permute-done.35.refs_4_ = bf16[384,768]{1,0:T(8,128)(2,1)S(1)} collective-permute-done((bf16[384,768]{1,0:T(8,128)(2,1)S(1)}, bf16[384,768]{1,0:T(8,128)(2,1)S(1)}, u32[]{:S(2)}, u32[]{:S(2)}) %collective-permute-start.35) | collective-permute-done | bytes 589856 | tf_op jit(solution)/shard_map/ppermute | solution.py:936
  219.6 2.1 place_rows.1
  221.6 5.4 %place_down.1 = (f32[3072,768]{1,0:T(8,128)}, f32[8,128]{1,0:T(8,128)S(1)}) custom-call(s32[4]{0:T(128)S(1)} %copy-done.6, bf16[4,384,768]{2,1,0:T(8,128)(2,1)S(1)} %get-tuple-element.200.refs_1_, bf16[4,384,768]{2,1,0:T(8,128)(2,1)S(1)} %collective-permute-done.39.refs_2_, f32[8,128]{1,0:T(8,128)S(1)} %get-tuple-element.201.refs_3_), custom_call_target="tpu_custom_call" | custom-call | flops 200000000 | bytes 1000 | tf_op jit(solution)/shard_map/place_down/pallas_call | solution.py:68
  227.1 5.4 %place_up.1 = (f32[768,3072]{1,0:T(8,128)}, f32[8,128]{1,0:T(8,128)S(1)}) custom-call(s32[4]{0:T(128)S(1)} %copy-done.6, bf16[4,384,768]{2,1,0:T(8,128)(2,1)S(1)} %get-tuple-element.199.refs_1_, bf16[4,384,768]{2,1,0:T(8,128)(2,1)S(1)} %collective-permute-done.38.refs_2_, f32[8,128]{1,0:T(8,128)S(1)} %get-tuple-element.202.refs_3_), custom_call_target="tpu_custom_call" | custom-call | flops 200000000 | bytes 1000 | tf_op jit(solution)/shard_map/place_up/pallas_call | solution.py:68
  241.5 4.4 %place_mixed.2 = (f32[768,2304]{1,0:T(8,128)}, f32[768,768]{1,0:T(8,128)}, f32[8,128]{1,0:T(8,128)S(1)}) custom-call(s32[4]{0:T(128)S(1)} %copy-done.6, bf16[3,384,768]{2,1,0:T(8,128)(2,1)S(1)} %get-tuple-element.206.refs_1_, bf16[3,384,768]{2,1,0:T(8,128)(2,1)S(1)} %collective-permute-done.42.refs_2_, f32[8,128]{1,0:T(8,128)S(1)} %copy-done.9), custom_call_target="tpu_custom_call" | custom-call | flops 200000000 | bytes 1000 | tf_op jit(solution)/shard_map/place_mixed/pallas_call | solution.py:68
  249.0 2.0 collective-permute-done.43.refs_2_
  251.0 2.9 %place_mixed.3 = (f32[768,2304]{1,0:T(8,128)}, f32[768,768]{1,0:T(8,128)}, f32[8,128]{1,0:T(8,128)}) custom-call(s32[4]{0:T(128)S(1)} %copy-done.6, bf16[2,192,768]{2,1,0:T(8,128)(2,1)S(1)} %get-tuple-element.209.refs_1_, bf16[2,192,768]{2,1,0:T(8,128)(2,1)S(1)} %collective-permute-done.43.refs_2_, ...), custom_call_target="tpu_custom_call", output_to_operand_aliasing={{0}: (3, {}), {1}: (4, {})} | custom-call | flops 200000000 | bytes 1000 | tf_op jit(solution)/shard_map/place_mixed/pallas_call | solution.py:68
  (196 shorter events, 74.9 us)
Async XLA Ops:
  2.7 12.9 %collective-permute-start = (bf16[2,128,768]{2,1,0:T(8,128)(2,1)S(1)}, bf16[2,128,768]{2,1,0:T(8,128)(2,1)S(1)}, u32[]{:S(2)}, u32[]{:S(2)}) collective-permute-start(bf16[2,128,768]{2,1,0:T(8,128)(2,1)S(1)} %get-tuple-element.227), channel_id=1, source_target_pairs={{0,16},{16,0},{1,17},{17,1},{2,18},{18,2},{3,19},{19,3},{4,20},{20... | collective-permute-start | bytes 1179656 | tf_op jit(solution)/shard_map/ppermute | solution.py:936
  7.6 15.6 %collective-permute-start.1 = (bf16[2,128,768]{2,1,0:T(8,128)(2,1)S(1)}, bf16[2,128,768]{2,1,0:T(8,128)(2,1)S(1)}, u32[]{:S(2)}, u32[]{:S(2)}) collective-permute-start(bf16[2,128,768]{2,1,0:T(8,128)(2,1)S(1)} %get-tuple-element.225), channel_id=1, source_target_pairs={{0,16},{16,0},{1,17},{17,1},{2,18},{18,2},{3,19},{19,3},{4,20},{20... | collective-permute-start | bytes 1179656 | tf_op jit(solution)/shard_map/ppermute | solution.py:936
  66.7 16.0 %collective-permute-start.2 = (bf16[2,128,768]{2,1,0:T(8,128)(2,1)}, bf16[2,128,768]{2,1,0:T(8,128)(2,1)S(1)}, u32[]{:S(2)}, u32[]{:S(2)}) collective-permute-start(bf16[2,128,768]{2,1,0:T(8,128)(2,1)} %get-tuple-element.117), channel_id=1, source_target_pairs={{0,16},{16,0},{1,17},{17,1},{2,18},{18,2},{3,19},{19,3},{4,20},{20... | collective-permute-start | bytes 1179656 | tf_op jit(solution)/shard_map/ppermute | solution.py:936
  68.5 14.2 %collective-permute-start.4 = (bf16[512,1536]{1,0:T(8,128)(2,1)}, bf16[512,1536]{1,0:T(8,128)(2,1)S(1)}, u32[]{:S(2)}, u32[]{:S(2)}) collective-permute-start(bf16[512,1536]{1,0:T(8,128)(2,1)} %get-tuple-element.129), channel_id=1, source_target_pairs={{0,1},{1,0},{2,3},{3,2},{4,5},{5,4},{6,7},{7,6},{8,9},{9,8},{10,11... | collective-permute-start | bytes 4718600 | tf_op jit(solution)/shard_map/ppermute | solution.py:934
  68.7 14.1 %collective-permute-start.3 = (bf16[3,512,768]{2,1,0:T(8,128)(2,1)}, bf16[3,512,768]{2,1,0:T(8,128)(2,1)S(1)}, u32[]{:S(2)}, u32[]{:S(2)}) collective-permute-start(bf16[3,512,768]{2,1,0:T(8,128)(2,1)} %get-tuple-element.127.refs_1_.refs_3_), channel_id=1, source_target_pairs={{0,1},{1,0},{2,3},{3,2},{4,5},{5,4},{6,7},{7,6},{8,9},{9,8},{10,11... | collective-permute-start | bytes 7077896 | tf_op jit(solution)/shard_map/ppermute | solution.py:934
  81.0 28.3 %collective-permute-start.8 = (bf16[2,384,768]{2,1,0:T(8,128)(2,1)}, bf16[2,384,768]{2,1,0:T(8,128)(2,1)}, u32[]{:S(2)}, u32[]{:S(2)}) collective-permute-start(bf16[2,384,768]{2,1,0:T(8,128)(2,1)} %get-tuple-element.141), channel_id=1, source_target_pairs={{0,2},{1,3},{2,0},{3,1},{4,6},{5,7},{6,4},{7,5},{8,10},{9,11},{10,... | collective-permute-start | bytes 3538952 | tf_op jit(solution)/shard_map/ppermute | solution.py:935
  87.8 28.9 %collective-permute-start.7 = (bf16[2,384,768]{2,1,0:T(8,128)(2,1)S(1)}, bf16[2,384,768]{2,1,0:T(8,128)(2,1)S(1)}, u32[]{:S(2)}, u32[]{:S(2)}) collective-permute-start(bf16[2,384,768]{2,1,0:T(8,128)(2,1)S(1)} %get-tuple-element.138), channel_id=1, source_target_pairs={{0,16},{16,0},{1,17},{17,1},{2,18},{18,2},{3,19},{19,3},{4,20},{20... | collective-permute-start | bytes 3538952 | tf_op jit(solution)/shard_map/ppermute | solution.py:936
  104.1 13.5 %collective-permute-start.11 = (bf16[512,1536]{1,0:T(8,128)(2,1)S(1)}, bf16[512,1536]{1,0:T(8,128)(2,1)S(1)}, u32[]{:S(2)}, u32[]{:S(2)}) collective-permute-start(bf16[512,1536]{1,0:T(8,128)(2,1)S(1)} %get-tuple-element.148), channel_id=1, source_target_pairs={{0,1},{1,0},{2,3},{3,2},{4,5},{5,4},{6,7},{7,6},{8,9},{9,8},{10,11... | collective-permute-start | bytes 4718600 | tf_op jit(solution)/shard_map/ppermute | solution.py:934
  111.1 18.2 %collective-permute-start.10 = (bf16[384,768]{1,0:T(8,128)(2,1)S(1)}, bf16[384,768]{1,0:T(8,128)(2,1)S(1)}, u32[]{:S(2)}, u32[]{:S(2)}) collective-permute-start(bf16[384,768]{1,0:T(8,128)(2,1)S(1)} %get-tuple-element.146), channel_id=1, source_target_pairs={{0,16},{16,0},{1,17},{17,1},{2,18},{18,2},{3,19},{19,3},{4,20},{20... | collective-permute-start | bytes 1769480 | tf_op jit(solution)/shard_map/ppermute | solution.py:936
  117.4 16.3 %collective-permute-start.9 = (bf16[384,768]{1,0:T(8,128)(2,1)S(1)}, bf16[384,768]{1,0:T(8,128)(2,1)S(1)}, u32[]{:S(2)}, u32[]{:S(2)}) collective-permute-start(bf16[384,768]{1,0:T(8,128)(2,1)S(1)} %get-tuple-element.144), channel_id=1, source_target_pairs={{0,2},{1,3},{2,0},{3,1},{4,6},{5,7},{6,4},{7,5},{8,10},{9,11},{10,... | collective-permute-start | bytes 1769480 | tf_op jit(solution)/shard_map/ppermute | solution.py:935
  123.8 13.0 %collective-permute-start.14 = (bf16[192,768]{1,0:T(8,128)(2,1)S(1)}, bf16[192,768]{1,0:T(8,128)(2,1)S(1)}, u32[]{:S(2)}, u32[]{:S(2)}) collective-permute-start(bf16[192,768]{1,0:T(8,128)(2,1)S(1)} %get-tuple-element.158), channel_id=1, source_target_pairs={{0,2},{1,3},{2,0},{3,1},{4,6},{5,7},{6,4},{7,5},{8,10},{9,11},{10,... | collective-permute-start | bytes 884744 | tf_op jit(solution)/shard_map/ppermute | solution.py:935
  125.7 11.1 %collective-permute-start.15 = (bf16[192,768]{1,0:T(8,128)(2,1)S(1)}, bf16[192,768]{1,0:T(8,128)(2,1)S(1)}, u32[]{:S(2)}, u32[]{:S(2)}) collective-permute-start(bf16[192,768]{1,0:T(8,128)(2,1)S(1)} %get-tuple-element.159), channel_id=1, source_target_pairs={{0,16},{16,0},{1,17},{17,1},{2,18},{18,2},{3,19},{19,3},{4,20},{20... | collective-permute-start | bytes 884744 | tf_op jit(solution)/shard_map/ppermute | solution.py:936
  131.3 8.4 %collective-permute-start.13 = (bf16[192,768]{1,0:T(8,128)(2,1)S(1)}, bf16[192,768]{1,0:T(8,128)(2,1)S(1)}, u32[]{:S(2)}, u32[]{:S(2)}) collective-permute-start(bf16[192,768]{1,0:T(8,128)(2,1)S(1)} %get-tuple-element.155), channel_id=1, source_target_pairs={{0,4},{1,5},{2,6},{3,7},{4,0},{5,1},{6,2},{7,3},{8,12},{9,13},{10,... | collective-permute-start | bytes 884744 | tf_op jit(solution)/shard_map/ppermute | solution.py:1009
  137.6 26.7 %collective-permute-start.20 = (bf16[384,768]{1,0:T(8,128)(2,1)S(1)}, bf16[384,768]{1,0:T(8,128)(2,1)S(1)}, u32[]{:S(2)}, u32[]{:S(2)}) collective-permute-start(bf16[384,768]{1,0:T(8,128)(2,1)S(1)} %get-tuple-element.170), channel_id=1, source_target_pairs={{0,2},{1,3},{2,0},{3,1},{4,6},{5,7},{6,4},{7,5},{8,10},{9,11},{10,... | collective-permute-start | bytes 1769480 | tf_op jit(solution)/shard_map/ppermute | solution.py:935
  137.9 26.3 %collective-permute-start.21 = (bf16[384,768]{1,0:T(8,128)(2,1)S(1)}, bf16[384,768]{1,0:T(8,128)(2,1)S(1)}, u32[]{:S(2)}, u32[]{:S(2)}) collective-permute-start(bf16[384,768]{1,0:T(8,128)(2,1)S(1)} %get-tuple-element.171), channel_id=1, source_target_pairs={{0,16},{16,0},{1,17},{17,1},{2,18},{18,2},{3,19},{19,3},{4,20},{20... | collective-permute-start | bytes 1769480 | tf_op jit(solution)/shard_map/ppermute | solution.py:936
  140.3 12.7 %collective-permute-start.16 = (bf16[192,768]{1,0:T(8,128)(2,1)S(1)}, bf16[192,768]{1,0:T(8,128)(2,1)S(1)}, u32[]{:S(2)}, u32[]{:S(2)}) collective-permute-start(bf16[192,768]{1,0:T(8,128)(2,1)S(1)} %get-tuple-element.162.refs_1_), channel_id=1, source_target_pairs={{0,8},{1,9},{2,10},{3,11},{4,12},{5,13},{6,14},{7,15},{8,0},{9,1},... | collective-permute-start | bytes 884744 | tf_op jit(solution)/shard_map/ppermute | solution.py:1010
  142.9 11.4 %collective-permute-start.12 = (bf16[192,768]{1,0:T(8,128)(2,1)S(1)}, bf16[192,768]{1,0:T(8,128)(2,1)S(1)}, u32[]{:S(2)}, u32[]{:S(2)}) collective-permute-start(bf16[192,768]{1,0:T(8,128)(2,1)S(1)} %get-tuple-element.153), channel_id=1, source_target_pairs={{0,4},{1,5},{2,6},{3,7},{4,0},{5,1},{6,2},{7,3},{8,12},{9,13},{10,... | collective-permute-start | bytes 884744 | tf_op jit(solution)/shard_map/ppermute | solution.py:1009
  144.5 25.0 %collective-permute-start.6 = (bf16[2,128,768]{2,1,0:T(8,128)(2,1)S(1)}, bf16[2,128,768]{2,1,0:T(8,128)(2,1)S(1)}, u32[]{:S(2)}, u32[]{:S(2)}) collective-permute-start(bf16[2,128,768]{2,1,0:T(8,128)(2,1)S(1)} %get-tuple-element.136), channel_id=1, source_target_pairs={{0,16},{16,0},{1,17},{17,1},{2,18},{18,2},{3,19},{19,3},{4,20},{20... | collective-permute-start | bytes 1179656 | tf_op jit(solution)/shard_map/ppermute | solution.py:936
  154.3 17.0 %collective-permute-start.19 = (bf16[192,768]{1,0:T(8,128)(2,1)S(1)}, bf16[192,768]{1,0:T(8,128)(2,1)S(1)}, u32[]{:S(2)}, u32[]{:S(2)}) collective-permute-start(bf16[192,768]{1,0:T(8,128)(2,1)S(1)} %get-tuple-element.168.refs_1_), channel_id=1, source_target_pairs={{0,4},{1,5},{2,6},{3,7},{4,0},{5,1},{6,2},{7,3},{8,12},{9,13},{10,... | collective-permute-start | bytes 884744 | tf_op jit(solution)/shard_map/ppermute | solution.py:1009
  166.9 14.5 %collective-permute-start.18 = (bf16[192,768]{1,0:T(8,128)(2,1)S(1)}, bf16[192,768]{1,0:T(8,128)(2,1)S(1)}, u32[]{:S(2)}, u32[]{:S(2)}) collective-permute-start(bf16[192,768]{1,0:T(8,128)(2,1)S(1)} %get-tuple-element.167.refs_1_), channel_id=1, source_target_pairs={{0,8},{1,9},{2,10},{3,11},{4,12},{5,13},{6,14},{7,15},{8,0},{9,1},... | collective-permute-start | bytes 884744 | tf_op jit(solution)/shard_map/ppermute | solution.py:1010
  171.9 14.9 %collective-permute-start.28 = (bf16[384,768]{1,0:T(8,128)(2,1)S(1)}, bf16[384,768]{1,0:T(8,128)(2,1)S(1)}, u32[]{:S(2)}, u32[]{:S(2)}) collective-permute-start(bf16[384,768]{1,0:T(8,128)(2,1)S(1)} %get-tuple-element.182.refs_1_), channel_id=1, source_target_pairs={{0,16},{16,0},{1,17},{17,1},{2,18},{18,2},{3,19},{19,3},{4,20},{20... | collective-permute-start | bytes 1769480 | tf_op jit(solution)/shard_map/ppermute | solution.py:936
  174.7 12.1 %collective-permute-start.27 = (bf16[384,768]{1,0:T(8,128)(2,1)S(1)}, bf16[384,768]{1,0:T(8,128)(2,1)S(1)}, u32[]{:S(2)}, u32[]{:S(2)}) collective-permute-start(bf16[384,768]{1,0:T(8,128)(2,1)S(1)} %get-tuple-element.182.refs_1_), channel_id=1, source_target_pairs={{0,2},{1,3},{2,0},{3,1},{4,6},{5,7},{6,4},{7,5},{8,10},{9,11},{10,... | collective-permute-start | bytes 1769480 | tf_op jit(solution)/shard_map/ppermute | solution.py:935
  190.5 16.3 %collective-permute-start.31 = (bf16[384,768]{1,0:T(8,128)(2,1)S(1)}, bf16[384,768]{1,0:T(8,128)(2,1)S(1)}, u32[]{:S(2)}, u32[]{:S(2)}) collective-permute-start(bf16[384,768]{1,0:T(8,128)(2,1)S(1)} %get-tuple-element.186.refs_1_), channel_id=1, source_target_pairs={{0,16},{16,0},{1,17},{17,1},{2,18},{18,2},{3,19},{19,3},{4,20},{20... | collective-permute-start | bytes 1769480 | tf_op jit(solution)/shard_map/ppermute | solution.py:936
  190.9 17.2 %collective-permute-start.30 = (bf16[384,768]{1,0:T(8,128)(2,1)S(1)}, bf16[384,768]{1,0:T(8,128)(2,1)S(1)}, u32[]{:S(2)}, u32[]{:S(2)}) collective-permute-start(bf16[384,768]{1,0:T(8,128)(2,1)S(1)} %get-tuple-element.186.refs_1_), channel_id=1, source_target_pairs={{0,2},{1,3},{2,0},{3,1},{4,6},{5,7},{6,4},{7,5},{8,10},{9,11},{10,... | collective-permute-start | bytes 1769480 | tf_op jit(solution)/shard_map/ppermute | solution.py:935
  192.4 15.7 %collective-permute-start.33 = (bf16[192,768]{1,0:T(8,128)(2,1)S(1)}, bf16[192,768]{1,0:T(8,128)(2,1)S(1)}, u32[]{:S(2)}, u32[]{:S(2)}) collective-permute-start(bf16[192,768]{1,0:T(8,128)(2,1)S(1)} %get-tuple-element.187.refs_1_), channel_id=1, source_target_pairs={{0,8},{1,9},{2,10},{3,11},{4,12},{5,13},{6,14},{7,15},{8,0},{9,1},... | collective-permute-start | bytes 884744 | tf_op jit(solution)/shard_map/ppermute | solution.py:1010
  193.1 22.2 %collective-permute-start.35 = (bf16[384,768]{1,0:T(8,128)(2,1)S(1)}, bf16[384,768]{1,0:T(8,128)(2,1)S(1)}, u32[]{:S(2)}, u32[]{:S(2)}) collective-permute-start(bf16[384,768]{1,0:T(8,128)(2,1)S(1)} %collective-permute-done.27.refs_4_.refs_2_), channel_id=1, source_target_pairs={{0,16},{16,0},{1,17},{17,1},{2,18},{18,2},{3,19},{19,3},{4,20},{20... | collective-permute-start | bytes 1769480 | tf_op jit(solution)/shard_map/ppermute | solution.py:936
  206.9 10.5 %collective-permute-start.32 = (bf16[384,768]{1,0:T(8,128)(2,1)S(1)}, bf16[384,768]{1,0:T(8,128)(2,1)S(1)}, u32[]{:S(2)}, u32[]{:S(2)}) collective-permute-start(bf16[384,768]{1,0:T(8,128)(2,1)S(1)} %collective-permute-done.31.refs_5_.refs_3_), channel_id=1, source_target_pairs={{0,2},{1,3},{2,0},{3,1},{4,6},{5,7},{6,4},{7,5},{8,10},{9,11},{10,... | collective-permute-start | bytes 1769480 | tf_op jit(solution)/shard_map/ppermute | solution.py:935
  218.0 9.0 %collective-permute-start.38 = (bf16[4,384,768]{2,1,0:T(8,128)(2,1)S(1)}, bf16[4,384,768]{2,1,0:T(8,128)(2,1)S(1)}, u32[]{:S(2)}, u32[]{:S(2)}) collective-permute-start(bf16[4,384,768]{2,1,0:T(8,128)(2,1)S(1)} %get-tuple-element.199.refs_1_), channel_id=1, source_target_pairs={{0,1},{1,0},{2,3},{3,2},{4,5},{5,4},{6,7},{7,6},{8,9},{9,8},{10,11... | collective-permute-start | bytes 7077896 | tf_op jit(solution)/shard_map/ppermute | solution.py:934
  218.6 15.3 %collective-permute-start.37 = (bf16[384,768]{1,0:T(8,128)(2,1)S(1)}, bf16[384,768]{1,0:T(8,128)(2,1)S(1)}, u32[]{:S(2)}, u32[]{:S(2)}) collective-permute-start(bf16[384,768]{1,0:T(8,128)(2,1)S(1)} %get-tuple-element.198.refs_1_), channel_id=1, source_target_pairs={{0,16},{16,0},{1,17},{17,1},{2,18},{18,2},{3,19},{19,3},{4,20},{20... | collective-permute-start | bytes 1769480 | tf_op jit(solution)/shard_map/ppermute | solution.py:936
  218.9 15.1 %collective-permute-start.36 = (bf16[384,768]{1,0:T(8,128)(2,1)S(1)}, bf16[384,768]{1,0:T(8,128)(2,1)S(1)}, u32[]{:S(2)}, u32[]{:S(2)}) collective-permute-start(bf16[384,768]{1,0:T(8,128)(2,1)S(1)} %get-tuple-element.198.refs_1_), channel_id=1, source_target_pairs={{0,2},{1,3},{2,0},{3,1},{4,6},{5,7},{6,4},{7,5},{8,10},{9,11},{10,... | collective-permute-start | bytes 1769480 | tf_op jit(solution)/shard_map/ppermute | solution.py:935
  236.1 9.9 %collective-permute-start.40 = (bf16[192,768]{1,0:T(8,128)(2,1)}, bf16[192,768]{1,0:T(8,128)(2,1)}, u32[]{:S(2)}, u32[]{:S(2)}) collective-permute-start(bf16[192,768]{1,0:T(8,128)(2,1)} %get-tuple-element.204), channel_id=1, source_target_pairs={{0,16},{16,0},{1,17},{17,1},{2,18},{18,2},{3,19},{19,3},{4,20},{20... | collective-permute-start | bytes 884744 | tf_op jit(solution)/shard_map/ppermute | solution.py:936
  237.8 9.5 %collective-permute-start.41 = (bf16[192,768]{1,0:T(8,128)(2,1)}, bf16[192,768]{1,0:T(8,128)(2,1)}, u32[]{:S(2)}, u32[]{:S(2)}) collective-permute-start(bf16[192,768]{1,0:T(8,128)(2,1)} %get-tuple-element.205), channel_id=1, source_target_pairs={{0,2},{1,3},{2,0},{3,1},{4,6},{5,7},{6,4},{7,5},{8,10},{9,11},{10,... | collective-permute-start | bytes 884744 | tf_op jit(solution)/shard_map/ppermute | solution.py:935
  (57 other events, 427.9 us)
